TPU v7x, 32 devices: a whole 2x2x4 slice. The times are simulated.
32 devices in a mesh: dp: 16 (over z, y, x), mp: 2 (over core).
Axes of the slice: x: 2, y: 2, z: 4, core: 2. Of those that a mesh axis runs over, the one named last changes fastest.
Arguments:
- media_feats: bfloat16 [2, 8192, 1536], P(None, ('dp', 'mp')), may hold values from -6 to 6
- latents: bfloat16 [2, 8192, 1536], P(None, ('dp', 'mp')), may hold values from -6 to 6
- patch_counts: int32 [2, 128], P(None, ('dp', 'mp')), may hold values from 1 to 253, as said below
- cotangent: bfloat16 [2, 8192, 1536], P(None, ('dp', 'mp')), may hold values from -6 to 6
- query_weight: bfloat16 [1536, 1536], replicated, may hold values from -0.15625 to 0.15625
- key_weight: bfloat16 [1536, 1536], replicated, may hold values from -0.15625 to 0.15625
- value_weight: bfloat16 [1536, 1536], replicated, may hold values from -0.15625 to 0.15625
- out_weight: bfloat16 [1536, 1536], replicated, may hold values from -0.625 to 0.625
- up_weight: bfloat16 [1536, 6144], P(None, 'mp'), may hold values from -0.15625 to 0.15625
- down_weight: bfloat16 [6144, 1536], P('mp'), may hold values from -0.078125 to 0.078125
- media_gain: float32 [1536], replicated, may hold values from 0.5 to 1.5
- media_shift: float32 [1536], replicated, may hold values from -3 to 3
- latent_gain: float32 [1536], replicated, may hold values from 0.5 to 1.5
- latent_shift: float32 [1536], replicated, may hold values from -3 to 3
- feed_gain: float32 [1536], replicated, may hold values from 0.5 to 1.5
- feed_shift: float32 [1536], replicated, may hold values from -3 to 3
Outputs:
- latents_out: bfloat16 [2, 8192, 1536], P(None, ('dp', 'mp'))
- grad_latents: float32 [2, 8192, 1536], P(None, ('dp', 'mp'))
- grad_media: float32 [2, 8192, 1536], P(None, ('dp', 'mp'))
- grad_query_weight: float32 [1536, 1536], P(('dp', 'mp'))
- grad_key_weight: float32 [1536, 1536], P(('dp', 'mp'))
- grad_value_weight: float32 [1536, 1536], P(('dp', 'mp'))
- grad_out_weight: float32 [1536, 1536], P(None, ('dp', 'mp'))
- grad_up_weight: float32 [1536, 6144], P('dp', 'mp')
- grad_down_weight: float32 [6144, 1536], P('mp', 'dp')
- grad_media_gain: float32 [1536], P(('dp', 'mp'))
- grad_media_shift: float32 [1536], P(('dp', 'mp'))
- grad_latent_gain: float32 [1536], P(('dp', 'mp'))
- grad_latent_shift: float32 [1536], P(('dp', 'mp'))
- grad_feed_gain: float32 [1536], P(('dp', 'mp'))
- grad_feed_shift: float32 [1536], P(('dp', 'mp'))
Inputs may be any that keep to these rules, and one draw needn't show every extreme that they name: `patch_counts`: entries 4 * k to 4 * k + 3 of a micro-batch are the images of one block of 256 patch rows; their counts sum to at most 256, exactly 256 in some block, and their patches fill the block's rows in order from its start. Some image has 253 patch rows.
All inputs are finite; a program needn't handle non-finite values.
Results may differ from a plain program's by a relative error of at most 0.014.
Values may be sent and summed in bfloat16 or wider, within the bound.
No kernel may reach another device: no remote copies, remote signals or barrier semaphores. Data moves between devices by JAX's collectives and lax.ppermute only.
A program may use at most 256 MiB of HBM per device.

v0:
```python
import jax
import jax.numpy as jnp
from jax import lax
from jax.sharding import PartitionSpec as P

HEADS = 16
LAT_IMG = 64


EPSILON = 1e-05
MASKED_SCORE = -1e30
ROOT_HALF = 0.7071067811865476
DENSITY_SCALE = 0.3989422804014327


def normalize(values, gain_vec, shift_vec):
    row_mean = jnp.mean(values, -1, keepdims=True)
    centred = values - row_mean
    inv_scale = lax.rsqrt(jnp.mean(centred * centred, -1, keepdims=True) + EPSILON)
    scaled = centred * inv_scale
    return (scaled * gain_vec + shift_vec, scaled, inv_scale)


def normalize_back(upstream, gain_vec, scaled, inv_scale):
    weighted = upstream * gain_vec
    first_mean = jnp.mean(weighted, -1, keepdims=True)
    second_mean = jnp.mean(weighted * scaled, -1, keepdims=True)
    grad_input = inv_scale * (weighted - first_mean - scaled * second_mean)
    return (grad_input, jnp.sum(upstream * scaled, 0), jnp.sum(upstream, 0))


def project(rows_low, weight):
    return jnp.dot(rows_low, weight, preferred_element_type=jnp.float32).astype(jnp.bfloat16)


def left_product(rows_low, grads_low):
    return jnp.einsum("rd,re->de", rows_low, grads_low, preferred_element_type=jnp.float32)


def back_product(grads_low, weight):
    return jnp.einsum("re,de->rd", grads_low, weight, preferred_element_type=jnp.float32)


def masked_scores(query_heads, key_heads, mask_table, scale):
    scores = (
        jnp.einsum("qhd,khd->hqk", query_heads, key_heads, preferred_element_type=jnp.float32)
        * scale
    )
    return jnp.where(mask_table[None], scores, MASKED_SCORE)


def micro_batch(media_feats, latents, patch_counts, cotangent, weights, norms):
    query_weight, key_weight, value_weight, out_weight, up_weight, down_weight = weights
    media_gain, media_shift, latent_gain, latent_shift, feed_gain, feed_shift = norms
    patches = media_feats.shape[0]
    latent_rows = latents.shape[0]
    model_width = latents.shape[1]
    head_dim = model_width // HEADS
    scale = head_dim ** (-0.5)
    latents_full = latents.astype(jnp.float32)
    media_n, media_hat, media_inv = normalize(
        media_feats.astype(jnp.float32), media_gain, media_shift
    )
    latent_n, latent_hat, latent_inv = normalize(latents_full, latent_gain, latent_shift)
    media_low = media_n.astype(jnp.bfloat16)
    latent_low = latent_n.astype(jnp.bfloat16)
    queries = project(latent_low, query_weight)
    key_media = project(media_low, key_weight)
    value_media = project(media_low, value_weight)
    key_latent = project(latent_low, key_weight)
    value_latent = project(latent_low, value_weight)
    image_ends = jnp.cumsum(patch_counts)
    positions = lax.iota(jnp.int32, patches)
    media_image = jnp.sum((positions[:, None] >= image_ends[None, :]).astype(jnp.int32), 1)
    latent_image = lax.iota(jnp.int32, latent_rows) // LAT_IMG
    key_image = jnp.concatenate([media_image, latent_image])
    mask_table = latent_image[:, None] == key_image[None, :]
    query_heads = queries.reshape(latent_rows, HEADS, head_dim)
    key_heads = jnp.concatenate([key_media, key_latent]).reshape(-1, HEADS, head_dim)
    value_heads = jnp.concatenate([value_media, value_latent]).reshape(-1, HEADS, head_dim)
    scores = masked_scores(query_heads, key_heads, mask_table, scale)
    row_max = jnp.max(scores, -1, keepdims=True)
    exp_scores = jnp.exp(scores - row_max)
    row_sum = jnp.sum(exp_scores, -1, keepdims=True)
    log_norm = row_max + jnp.log(row_sum)
    probs_low = (exp_scores / row_sum).astype(jnp.bfloat16)
    mixed_out = jnp.einsum(
        "hqk,khd->qhd", probs_low, value_heads, preferred_element_type=jnp.float32
    )
    mixed_low = mixed_out.reshape(latent_rows, model_width).astype(jnp.bfloat16)
    residual = latents_full + jnp.dot(mixed_low, out_weight, preferred_element_type=jnp.float32)
    feed_in, feed_hat, feed_inv = normalize(residual, feed_gain, feed_shift)
    feed_low = feed_in.astype(jnp.bfloat16)
    feed_all = lax.all_gather(feed_low, "mp", axis=0, tiled=True)
    up_proj = jnp.dot(feed_all, up_weight, preferred_element_type=jnp.float32)
    hidden = jax.nn.gelu(up_proj, approximate=False).astype(jnp.bfloat16)
    branch = lax.psum_scatter(
        jnp.dot(hidden, down_weight, preferred_element_type=jnp.float32).astype(jnp.bfloat16),
        "mp",
        scatter_dimension=0,
        tiled=True,
    ).astype(jnp.float32)
    result = (residual + branch).astype(jnp.bfloat16)
    grad_all = lax.all_gather(cotangent, "mp", axis=0, tiled=True)
    grad_down_w = jnp.einsum("rf,rd->fd", hidden, grad_all, preferred_element_type=jnp.float32)
    grad_hidden = jnp.einsum("rd,fd->rf", grad_all, down_weight, preferred_element_type=jnp.float32)
    normal_cdf = 0.5 * (1.0 + lax.erf(up_proj * ROOT_HALF))
    normal_pdf = jnp.exp(-0.5 * up_proj * up_proj) * DENSITY_SCALE
    grad_up = (grad_hidden * (normal_cdf + up_proj * normal_pdf)).astype(jnp.bfloat16)
    grad_up_w = jnp.einsum("rd,rf->df", feed_all, grad_up, preferred_element_type=jnp.float32)
    grad_feed_in = lax.psum_scatter(
        jnp.einsum("rf,df->rd", grad_up, up_weight, preferred_element_type=jnp.float32),
        "mp",
        scatter_dimension=0,
        tiled=True,
    )
    grad_feed_part, grad_feed_gain, grad_feed_shift = normalize_back(
        grad_feed_in, feed_gain, feed_hat, feed_inv
    )
    grad_residual = cotangent.astype(jnp.float32) + grad_feed_part
    grad_residual_low = grad_residual.astype(jnp.bfloat16)
    grad_out_w = left_product(mixed_low, grad_residual_low)
    grad_mixed = back_product(grad_residual_low, out_weight).astype(jnp.bfloat16)
    grad_mixed_heads = grad_mixed.reshape(latent_rows, HEADS, head_dim)
    again = masked_scores(query_heads, key_heads, mask_table, scale)
    attn_probs = jnp.where(mask_table[None], jnp.exp(again - log_norm), 0.0)
    again_low = attn_probs.astype(jnp.bfloat16)
    grad_values = jnp.einsum(
        "hqk,qhd->khd", again_low, grad_mixed_heads, preferred_element_type=jnp.float32
    )
    grad_probs = jnp.einsum(
        "qhd,khd->hqk", grad_mixed_heads, value_heads, preferred_element_type=jnp.float32
    )
    grad_scores = attn_probs * (grad_probs - jnp.sum(grad_probs * attn_probs, -1, keepdims=True))
    grad_scores_low = grad_scores.astype(jnp.bfloat16)
    grad_queries = (
        jnp.einsum("hqk,khd->qhd", grad_scores_low, key_heads, preferred_element_type=jnp.float32)
        * scale
    )
    grad_keys = (
        jnp.einsum("hqk,qhd->khd", grad_scores_low, query_heads, preferred_element_type=jnp.float32)
        * scale
    )
    grad_queries = grad_queries.reshape(latent_rows, model_width).astype(jnp.bfloat16)
    grad_keys = grad_keys.reshape(-1, model_width).astype(jnp.bfloat16)
    grad_values = grad_values.reshape(-1, model_width).astype(jnp.bfloat16)
    grad_key_media = grad_keys[:patches]
    grad_key_latent = grad_keys[patches:]
    grad_value_media = grad_values[:patches]
    grad_value_latent = grad_values[patches:]
    grad_query_w = left_product(latent_low, grad_queries)
    grad_key_w = left_product(media_low, grad_key_media) + left_product(latent_low, grad_key_latent)
    grad_value_w = left_product(media_low, grad_value_media) + left_product(
        latent_low, grad_value_latent
    )
    grad_latent_n = (
        back_product(grad_queries, query_weight)
        + back_product(grad_key_latent, key_weight)
        + back_product(grad_value_latent, value_weight)
    )
    grad_media_n = back_product(grad_key_media, key_weight) + back_product(
        grad_value_media, value_weight
    )
    grad_latent_part, grad_latent_gain, grad_latent_shift = normalize_back(
        grad_latent_n, latent_gain, latent_hat, latent_inv
    )
    grad_media, grad_media_gain, grad_media_shift = normalize_back(
        grad_media_n, media_gain, media_hat, media_inv
    )
    grad_latents = grad_residual + grad_latent_part
    attention_terms = (
        grad_query_w,
        grad_key_w,
        grad_value_w,
        grad_out_w,
        grad_media_gain,
        grad_media_shift,
        grad_latent_gain,
        grad_latent_shift,
        grad_feed_gain,
        grad_feed_shift,
    )
    feed_terms = (grad_up_w, grad_down_w)
    return (result, grad_latents, grad_media, attention_terms, feed_terms)


def add_terms(running, fresh):
    if running is None:
        return fresh
    return tuple((left_term + right_term for left_term, right_term in zip(running, fresh)))


def local(
    media_feats,
    latents,
    patch_counts,
    cotangent,
    query_weight,
    key_weight,
    value_weight,
    out_weight,
    up_weight,
    down_weight,
    media_gain,
    media_shift,
    latent_gain,
    latent_shift,
    feed_gain,
    feed_shift,
):
    weights = (query_weight, key_weight, value_weight, out_weight, up_weight, down_weight)
    norms = (media_gain, media_shift, latent_gain, latent_shift, feed_gain, feed_shift)
    outputs = []
    latent_grads = []
    media_grads = []
    attention_total = None
    feed_total = None
    for micro_step in range(media_feats.shape[0]):
        result, grad_latents, grad_media, attention_terms, feed_terms = micro_batch(
            media_feats[micro_step],
            latents[micro_step],
            patch_counts[micro_step],
            cotangent[micro_step],
            weights,
            norms,
        )
        outputs.append(result)
        latent_grads.append(grad_latents)
        media_grads.append(grad_media)
        attention_total = add_terms(attention_total, attention_terms)
        feed_total = add_terms(feed_total, feed_terms)
    term_q, term_k, term_v, term_o, term_mg, term_ms, term_lg, term_ls, term_fg, term_fs = (
        attention_total
    )
    attention_total = (
        lax.psum_scatter(term_q, ("dp", "mp"), scatter_dimension=0, tiled=True),
        lax.psum_scatter(term_k, ("dp", "mp"), scatter_dimension=0, tiled=True),
        lax.psum_scatter(term_v, ("dp", "mp"), scatter_dimension=0, tiled=True),
        lax.psum_scatter(term_o, ("dp", "mp"), scatter_dimension=1, tiled=True),
        lax.psum_scatter(term_mg, ("dp", "mp"), scatter_dimension=0, tiled=True),
        lax.psum_scatter(term_ms, ("dp", "mp"), scatter_dimension=0, tiled=True),
        lax.psum_scatter(term_lg, ("dp", "mp"), scatter_dimension=0, tiled=True),
        lax.psum_scatter(term_ls, ("dp", "mp"), scatter_dimension=0, tiled=True),
        lax.psum_scatter(term_fg, ("dp", "mp"), scatter_dimension=0, tiled=True),
        lax.psum_scatter(term_fs, ("dp", "mp"), scatter_dimension=0, tiled=True),
    )
    term_up, term_down = feed_total
    feed_total = (
        lax.psum_scatter(term_up, "dp", scatter_dimension=0, tiled=True),
        lax.psum_scatter(term_down, "dp", scatter_dimension=1, tiled=True),
    )
    return (
        jnp.stack(outputs),
        jnp.stack(latent_grads),
        jnp.stack(media_grads),
        attention_total[0],
        attention_total[1],
        attention_total[2],
        attention_total[3],
        feed_total[0],
        feed_total[1],
        attention_total[4],
        attention_total[5],
        attention_total[6],
        attention_total[7],
        attention_total[8],
        attention_total[9],
    )


def solution(mesh):
    in_specs = (
        P(None, ("dp", "mp"), None),
        P(None, ("dp", "mp"), None),
        P(None, ("dp", "mp")),
        P(None, ("dp", "mp"), None),
        P(),
        P(),
        P(),
        P(),
        P(None, "mp"),
        P("mp", None),
        P(),
        P(),
        P(),
        P(),
        P(),
        P(),
    )
    out_specs = (
        P(None, ("dp", "mp"), None),
        P(None, ("dp", "mp"), None),
        P(None, ("dp", "mp"), None),
        P(("dp", "mp"), None),
        P(("dp", "mp"), None),
        P(("dp", "mp"), None),
        P(None, ("dp", "mp")),
        P("dp", "mp"),
        P("mp", "dp"),
        P(("dp", "mp")),
        P(("dp", "mp")),
        P(("dp", "mp")),
        P(("dp", "mp")),
        P(("dp", "mp")),
        P(("dp", "mp")),
    )
    return jax.shard_map(local, mesh=mesh, in_specs=in_specs, out_specs=out_specs, check_vma=False)
```

profile of v0, /device:TPU:0, one launch (start us, length us, event | category | flops | bytes accessed | tf_op | source)
XLA Modules:
  0.0 1418.2 jit_solution(3153218811734635664)
XLA Ops:
  87.4 9.9 all-gather.7.cloned.1.call-done
  97.3 21.2 %fusion.6 = (bf16[512,3072]{1,0:T(8,128)(2,1)}, f32[512,3072]{1,0:T(8,128)}) fusion(bf16[512,1536]{1,0:T(8,128)(2,1)} %all-gather.7.cloned.1.call-done, bf16[1536,3072]{1,0:T(8,128)(2,1)} %param.24), kind=kOutput, calls=%fused_computation.30 | convolution fusion | flops 4934074368 | bytes 20447232 | tf_op jit(solution)/shard_map/dot_general | solution.py:95
  118.5 10.9 fusion.15
  131.1 9.7 fusion.196
  140.8 21.4 %fusion.9 = (bf16[512,3072]{1,0:T(8,128)(2,1)S(1)}, f32[512,3072]{1,0:T(8,128)}) fusion(bf16[512,1536]{1,0:T(8,128)(2,1)} %all-gather.9.cloned.1.call-done, bf16[1536,3072]{1,0:T(8,128)(2,1)} %param.24), kind=kOutput, calls=%fused_computation.33 | convolution fusion | flops 4934074368 | bytes 20447232 | tf_op jit(solution)/shard_map/dot_general | solution.py:95
  162.2 11.3 fusion.21
  175.2 9.2 fusion.198
  184.6 8.9 convolution_convert_fusion
  193.6 11.1 convolution_convert_fusion.1
  210.0 11.9 reduce-scatter.11.cloned.1.call-done
  232.3 7.2 multiply_reduce_fusion
  248.7 6.5 multiply_reduce_fusion.1
  286.5 6.5 fusion.127
  294.1 6.0 fusion.130
  320.0 12.0 fusion.202
  331.9 13.0 convolution_add_fusion.1
  345.3 11.2 fusion.122
  356.5 13.2 convolution_add_fusion
  399.8 41.6 %all-reduce.6 = (f32[1536]{0:T(1024)S(1)}, f32[1536]{0:T(1024)S(1)}, f32[1536]{0:T(1024)S(1)}, f32[1536]{0:T(1024)S(1)}, f32[1536]{0:T(1024)S(1)}, /*index=5*/f32[1536]{0:T(1024)S(1)}) all-reduce(f32[1536]{0:T(1024)S(1)} %add.301, f32[1536]{0:T(1024)S(1)} %add.302, ...), channel_id=14, replica_groups=mesh['dp'=16,'mp'=2] {'dp','mp'}, use_global_device_ids=true, to_apply=%region_46.47.clone | all-reduce | flops 9216 | bytes 73728
  456.6 90.0 %reduce-scatter.21.cloned.1.call-done = f32[48,1536]{1,0:T(8,128)} async-done(((f32[1536,1536]{1,0:T(8,128)}), f32[48,1536]{1,0:T(8,128)}) %reduce-scatter.21.cloned.1.call-update) | async-done | bytes 294928 | tf_op jit(solution)/shard_map/reduce_scatter | solution.py:237
  546.6 141.1 %reduce-scatter.23.cloned.1.call-done = f32[48,1536]{1,0:T(8,128)} async-done(((f32[1536,1536]{1,0:T(8,128)}), f32[48,1536]{1,0:T(8,128)}) %reduce-scatter.23.cloned.1.call-update) | async-done | bytes 294928 | tf_op jit(solution)/shard_map/reduce_scatter | solution.py:238
  687.8 141.9 %reduce-scatter.25.cloned.1.call-done = f32[1536,48]{0,1:T(8,128)} async-done(((f32[1536,1536]{0,1:T(8,128)}), f32[1536,48]{0,1:T(8,128)}) %reduce-scatter.25.cloned.1.call-update) | async-done | bytes 294928 | tf_op jit(solution)/shard_map/reduce_scatter | solution.py:239
  829.7 291.0 %reduce-scatter.27.cloned.1.call-done = f32[96,3072]{1,0:T(8,128)} async-done(((f32[1536,3072]{1,0:T(8,128)}), f32[96,3072]{1,0:T(8,128)}) %reduce-scatter.27.cloned.1.call-update) | async-done | bytes 1179664 | tf_op jit(solution)/shard_map/reduce_scatter | solution.py:249
  1120.7 290.5 %reduce-scatter.29.cloned.1.call-done = f32[3072,96]{0,1:T(8,128)} async-done(((f32[3072,1536]{0,1:T(8,128)}), f32[3072,96]{0,1:T(8,128)}) %reduce-scatter.29.cloned.1.call-update) | async-done | bytes 1179664 | tf_op jit(solution)/shard_map/reduce_scatter | solution.py:250
  (450 shorter events, 204.5 us)
Async XLA Ops:
  7.2 90.1 %all-gather.7.cloned.1.call-start = ((), (), s32[]{:S(2)}) async-start(), calls=%async_computation.10 | async-start | bytes 2359296 | tf_op jit(solution)/shard_map/all_gather | solution.py:94
  9.1 19.0 %copy-start.100 = (f32[256]{0:T(256)}, f32[256]{0:T(256)S(1)}, u32[]{:S(2)}) copy-start(f32[256]{0:T(256)S(1)} %get-tuple-element.105) | copy-start | bytes 3076
  10.0 22.7 %copy-start.90 = (f32[256]{0:T(256)}, f32[256]{0:T(256)S(1)}, u32[]{:S(2)}) copy-start(f32[256]{0:T(256)S(1)} %get-tuple-element.107) | copy-start | bytes 3076
  43.1 31.8 %copy-start.53 = (pred[256,512]{1,0:T(8,128)(4,1)}, pred[256,512]{1,0:T(8,128)(4,1)S(1)}, u32[]{:S(2)}) copy-start(pred[256,512]{1,0:T(8,128)(4,1)S(1)} %get-tuple-element.82) | copy-start | bytes 393220
  55.7 26.7 %copy-start.6 = (f32[256,1536]{1,0:T(8,128)}, f32[256,1536]{1,0:T(8,128)S(1)}, u32[]{:S(2)}) copy-start(f32[256,1536]{1,0:T(8,128)S(1)} %get-tuple-element.90) | copy-start | bytes 4718596
  55.8 26.7 %copy-start.106 = (f32[256]{0:T(256)}, f32[256]{0:T(256)S(1)}, u32[]{:S(2)}) copy-start(f32[256]{0:T(256)S(1)} %broadcast_multiply_fusion.15) | copy-start | bytes 3076
  57.7 24.8 %copy-start.112 = (f32[256]{0:T(256)}, f32[256]{0:T(256)S(1)}, u32[]{:S(2)}) copy-start(f32[256]{0:T(256)S(1)} %add_rsqrt_fusion.3) | copy-start | bytes 3076
  84.7 33.9 %all-gather.11.cloned.1.call-start = ((), (), s32[]{:S(2)}) async-start(), calls=%async_computation.22 | async-start | bytes 2359296 | tf_op jit(solution)/shard_map/all_gather | solution.py:104
  86.0 54.8 %all-gather.9.cloned.1.call-start = ((), (), s32[]{:S(2)}) async-start(), calls=%async_computation.12 | async-start | bytes 2359296 | tf_op jit(solution)/shard_map/all_gather | solution.py:94
  86.8 75.5 %all-gather.13.cloned.1.call-start = ((), (), s32[]{:S(2)}) async-start(), calls=%async_computation.23 | async-start | bytes 2359296 | tf_op jit(solution)/shard_map/all_gather | solution.py:104
  87.3 118.1 %reduce-scatter.15.cloned.1.call-start = ((), (), s32[]{:S(2)}) async-start(), calls=%async_computation.14 | async-start | bytes 4718592 | tf_op jit(solution)/shard_map/reduce_scatter | solution.py:111
  140.8 64.7 %reduce-scatter.17.cloned.1.call-start = ((), (), s32[]{:S(2)}) async-start(), calls=%async_computation.15 | async-start | bytes 4718592 | tf_op jit(solution)/shard_map/reduce_scatter | solution.py:111
  162.2 22.3 %copy-start.27 = (bf16[512,3072]{1,0:T(8,128)(2,1)}, bf16[512,3072]{1,0:T(8,128)(2,1)S(1)}, u32[]{:S(2)}) copy-start(bf16[512,3072]{1,0:T(8,128)(2,1)S(1)} %get-tuple-element.95) | copy-start | bytes 9437188
  184.5 25.5 %reduce-scatter.13.cloned.1.call-start = ((), (), s32[]{:S(2)}) async-start(), calls=%async_computation.13 | async-start | bytes 2359296 | tf_op jit(solution)/shard_map/reduce_scatter | solution.py:97
  193.5 28.4 %reduce-scatter.11.cloned.1.call-start = ((), (), s32[]{:S(2)}) async-start(), calls=%async_computation.11 | async-start | bytes 2359296 | tf_op jit(solution)/shard_map/reduce_scatter | solution.py:97
  204.8 251.9 %reduce-scatter.19.cloned.1.call-start = ((), (), s32[]{:S(2)}) async-start(), calls=%async_computation.16 | async-start | bytes 9732096 | tf_op jit(solution)/shard_map/reduce_scatter | solution.py:236
  244.3 18.1 %copy-start.29 = (bf16[16,96,256]{2,1,0:T(8,128)(2,1)}, bf16[16,96,256]{2,1,0:T(8,128)(2,1)S(1)}, u32[]{:S(2)}) copy-start(bf16[16,96,256]{2,1,0:T(8,128)(2,1)S(1)} %multiply_convert_fusion.4) | copy-start | bytes 2359300
  267.7 278.9 %reduce-scatter.21.cloned.1.call-start = ((), (), s32[]{:S(2)}) async-start(), calls=%async_computation.17 | async-start | bytes 9732096 | tf_op jit(solution)/shard_map/reduce_scatter | solution.py:237
  286.0 401.7 %reduce-scatter.23.cloned.1.call-start = ((), (), s32[]{:S(2)}) async-start(), calls=%async_computation.18 | async-start | bytes 9732096 | tf_op jit(solution)/shard_map/reduce_scatter | solution.py:238
  311.3 518.4 %reduce-scatter.25.cloned.1.call-start = ((), (), s32[]{:S(2)}) async-start(), calls=%async_computation.19 | async-start | bytes 9732096 | tf_op jit(solution)/shard_map/reduce_scatter | solution.py:239
  319.9 800.8 %reduce-scatter.27.cloned.1.call-start = ((), (), s32[]{:S(2)}) async-start(), calls=%async_computation.20 | async-start | bytes 20054016 | tf_op jit(solution)/shard_map/reduce_scatter | solution.py:249
  319.9 12.0 copy-start.36
  345.0 1066.2 %reduce-scatter.29.cloned.1.call-start = ((), (), s32[]{:S(2)}) async-start(), calls=%async_computation.21 | async-start | bytes 20054016 | tf_op jit(solution)/shard_map/reduce_scatter | solution.py:250
  369.7 12.2 slice-start.20
  (131 other events, 507.3 us)
Sparse Core Ops, SparseCore 0:
  84.8 12.5 all-gather.6
  99.4 10.9 all-gather.10
  112.0 10.9 all-gather.8
  124.4 10.9 all-gather.12
  140.9 12.0 reduce-scatter.14
  184.6 12.0 reduce-scatter.16
  199.0 10.2 reduce-scatter.12
  211.6 10.2 reduce-scatter.10
  267.8 136.8 reduce-scatter.18
  412.1 134.5 reduce-scatter.20
  553.1 134.6 reduce-scatter.22
  695.1 134.5 reduce-scatter.24
  836.0 284.5 reduce-scatter.26
  1126.9 284.2 reduce-scatter.28
where the time goes:
time: 1430 us; the launch traced here: 1420 us
  waiting for transfers between devices  978 us (68%)
  matrix products  298 us (21%)
  local copies, waits for them, and re-layouts  42.2 us (3%)
  blocking collectives  41.6 us (3%)
  other arithmetic  40.5 us (3%)
  between operations  16.5 us (1%)
    reduce_scatter x1, waiting for transfers between devices, local(): lax.psum_scatter(term_up, 'dp', scatter_dimension=0, tiled=True)  291 us
    reduce_scatter x1, waiting for transfers between devices, local(): lax.psum_scatter(term_down, 'dp', scatter_dimension=1, tiled=True)  291 us
    reduce_scatter x1, waiting for transfers between devices, local(): lax.psum_scatter(term_o, ('dp', 'mp'), scatter_dimension=1, tiled=True)  142 us
    reduce_scatter x1, waiting for transfers between devices, local(): lax.psum_scatter(term_v, ('dp', 'mp'), scatter_dimension=0, tiled=True)  141 us
    reduce_scatter x1, waiting for transfers between devices, local(): lax.psum_scatter(term_k, ('dp', 'mp'), scatter_dimension=0, tiled=True)  90 us
    dot_general x2, matrix products, micro_batch(): up_proj = jnp.dot(feed_all, up_weight, preferred_element_type=jnp.float32)  42.6 us
    unnamed x1, blocking collectives  41.6 us
    dot_general x12, matrix products, left_product(): jnp.einsum('rd,re->de', rows_low, grads_low, preferred_element_type=jnp.f...  35.5 us
  transfers between devices with their start and end apart: 14, of which 7 were waited for; matrix products, arithmetic and copies ran while one was open for 18% of the time, Pallas kernels for 0%

commit v1 on v0

v1 whole, which is shorter than its diff:
```python
import jax
import jax.numpy as jnp
from jax import lax
from jax.sharding import PartitionSpec as P

HEADS = 16
LAT_IMG = 64
EPSILON = 1e-05
MASKED_SCORE = -1e30
ROOT_HALF = 0.7071067811865476
DENSITY_SCALE = 0.3989422804014327
F32 = jnp.float32
BF16 = jnp.bfloat16


def normalize(values, gain_vec, shift_vec):
    row_mean = jnp.mean(values, -1, keepdims=True)
    centred = values - row_mean
    inv_scale = lax.rsqrt(jnp.mean(centred * centred, -1, keepdims=True) + EPSILON)
    scaled = centred * inv_scale
    return (scaled * gain_vec + shift_vec, scaled, inv_scale)


def normalize_back(upstream, gain_vec, scaled, inv_scale):
    weighted = upstream * gain_vec
    first_mean = jnp.mean(weighted, -1, keepdims=True)
    second_mean = jnp.mean(weighted * scaled, -1, keepdims=True)
    grad_input = inv_scale * (weighted - first_mean - scaled * second_mean)
    return (grad_input, jnp.sum(upstream * scaled, 0), jnp.sum(upstream, 0))


def dot(left, right):
    return jnp.dot(left, right, preferred_element_type=F32)


def dot_t(left, right):
    return jnp.einsum("rd,ed->re", left, right, preferred_element_type=F32)


def masked_scores(query_heads, key_heads, mask_table, scale):
    scores = jnp.einsum("qhd,khd->hqk", query_heads, key_heads, preferred_element_type=F32) * scale
    return jnp.where(mask_table[None], scores, MASKED_SCORE)


def mask_of(patch_counts, patches, latent_rows):
    images = patch_counts.shape[0]
    upto = lax.iota(jnp.int32, images)[:, None] >= lax.iota(jnp.int32, images)[None, :]
    image_ends = jnp.sum(jnp.where(upto, patch_counts[None, :], 0), 1)
    positions = lax.iota(jnp.int32, patches)
    media_image = jnp.sum((positions[:, None] >= image_ends[None, :]).astype(jnp.int32), 1)
    latent_image = lax.iota(jnp.int32, latent_rows) // LAT_IMG
    key_image = jnp.concatenate([media_image, latent_image])
    return latent_image[:, None] == key_image[None, :]


def attend(queries, keys, values, mask_table, scale):
    rows, width = queries.shape
    query_heads = queries.reshape(rows, HEADS, -1)
    key_heads = keys.reshape(keys.shape[0], HEADS, -1)
    value_heads = values.reshape(keys.shape[0], HEADS, -1)
    scores = masked_scores(query_heads, key_heads, mask_table, scale)
    row_max = jnp.max(scores, -1, keepdims=True)
    exp_scores = jnp.exp(scores - row_max)
    row_sum = jnp.sum(exp_scores, -1, keepdims=True)
    log_norm = row_max + jnp.log(row_sum)
    probs_low = (exp_scores / row_sum).astype(BF16)
    mixed = jnp.einsum("hqk,khd->qhd", probs_low, value_heads, preferred_element_type=F32)
    return mixed.reshape(rows, width).astype(BF16), log_norm


def attend_back(queries, keys, values, mask_table, scale, log_norm, grad_mixed):
    rows, width = queries.shape
    query_heads = queries.reshape(rows, HEADS, -1)
    key_heads = keys.reshape(keys.shape[0], HEADS, -1)
    value_heads = values.reshape(keys.shape[0], HEADS, -1)
    grad_heads = grad_mixed.reshape(rows, HEADS, -1)
    again = masked_scores(query_heads, key_heads, mask_table, scale)
    probs = jnp.where(mask_table[None], jnp.exp(again - log_norm), 0.0)
    probs_low = probs.astype(BF16)
    grad_values = jnp.einsum("hqk,qhd->khd", probs_low, grad_heads, preferred_element_type=F32)
    grad_probs = jnp.einsum("qhd,khd->hqk", grad_heads, value_heads, preferred_element_type=F32)
    grad_scores = probs * (grad_probs - jnp.sum(grad_probs * probs, -1, keepdims=True))
    grad_low = grad_scores.astype(BF16)
    grad_queries = jnp.einsum("hqk,khd->qhd", grad_low, key_heads, preferred_element_type=F32)
    grad_keys = jnp.einsum("hqk,qhd->khd", grad_low, query_heads, preferred_element_type=F32)
    return (
        (grad_queries * scale).reshape(rows, width).astype(BF16),
        (grad_keys * scale).reshape(-1, width).astype(BF16),
        grad_values.reshape(-1, width).astype(BF16),
    )


def bit_orders(count):
    bits = count.bit_length() - 1
    if bits == 4:
        return [(0, 1, 2, 3), (1, 0, 2, 3), (2, 3, 0, 1)]
    plain = tuple(range(bits))
    third = bits // 3
    return [plain[s:] + plain[:s] for s in (0, third, 2 * third)]


def sided(value, bit, bits, side):
    place = bits.index(bit)
    shape = value.shape
    outer = 1 << place
    parts = value.reshape((outer, 2, shape[0] // (2 * outer)) + shape[1:])
    return lax.dynamic_index_in_dim(parts, side, 1, keepdims=False).reshape((shape[0] // 2,) + shape[1:])


def swap_mp(value, size):
    return lax.ppermute(value, "mp", [(i, i ^ 1) for i in range(size)])


def steps_of(order, with_mp):
    if with_mp:
        return [("mp", 0)] + [("dp", bit + 1) for bit in order]
    return [("dp", bit) for bit in order]


def exchange(value, axis, bit, shifted, sizes):
    flip = 1 if axis == "mp" else 1 << (bit - shifted)
    return lax.ppermute(value, axis, [(i, i ^ flip) for i in range(sizes[axis])])


def halving(terms, bits, steps, block_index, shifted, sizes):
    for axis, bit in steps:
        mine = (block_index >> bit) & 1
        rear = [sided(t, bit, bits, 1 - mine) for t in terms]
        sent = rear[0] if len(rear) == 1 else sum(t.astype(F32) for t in rear).astype(rear[0].dtype)
        got = exchange(sent, axis, bit, shifted, sizes)
        terms = [sided(t, bit, bits, mine) for t in terms] + [got]
        bits = [b for b in bits if b != bit]
    return sum(t[0].astype(F32) for t in terms)


def scatter_product(left_t, right, cuts, orders, block_index, with_mp, sizes):
    blocks = sizes["dp"] * (sizes["mp"] if with_mp else 1)
    width = left_t.shape[0]
    shifted = 1 if with_mp else 0
    all_bits = list(range(blocks.bit_length() - 1))[::-1]
    parted = left_t.reshape(blocks, width // blocks, -1)
    pieces = []
    start = 0
    for cut, order in zip(cuts, orders):
        part = right[:, start : start + cut]
        steps = steps_of(order, with_mp)
        axis, bit = steps[0]
        mine = (block_index >> bit) & 1

        def half(side):
            rows = sided(parted, bit, all_bits, side).reshape(width // 2, -1)
            return dot(rows, part).astype(BF16).reshape(blocks // 2, width // blocks, cut)

        got = exchange(half(1 - mine), axis, bit, shifted, sizes)
        left_bits = [b for b in all_bits if b != bit]
        pieces.append(halving([half(mine), got], left_bits, steps[1:], block_index, shifted, sizes))
        start += cut
    return jnp.concatenate(pieces, 1)


def small_sums(vectors, block_index, order, sizes):
    blocks = sizes["dp"] * sizes["mp"]
    count = len(vectors)
    stacked = jnp.stack(vectors).reshape(count, blocks, -1).transpose(1, 0, 2)
    all_bits = list(range(blocks.bit_length() - 1))[::-1]
    share = halving([stacked], all_bits, steps_of(order, True), block_index, 1, sizes)
    return [share[i] for i in range(count)]


def cut_widths(width, shares):
    unit = 128
    total = width // unit
    whole = sum(shares)
    first = total * shares[0] // whole
    second = total * (shares[0] + shares[1]) // whole - first
    return [first * unit, second * unit, (total - first - second) * unit]


def build(dp_size, mp_size):
    orders = bit_orders(dp_size)
    sizes = {"dp": dp_size, "mp": mp_size}

    def local(
        media_feats,
        latents,
        patch_counts,
        cotangent,
        query_weight,
        key_weight,
        value_weight,
        out_weight,
        up_weight,
        down_weight,
        media_gain,
        media_shift,
        latent_gain,
        latent_shift,
        feed_gain,
        feed_shift,
    ):
        micro, patches, width = media_feats.shape
        latent_rows = latents.shape[1]
        scale = (width // HEADS) ** (-0.5)
        dp_index = lax.axis_index("dp").astype(jnp.int32)
        flat_index = dp_index * mp_size + lax.axis_index("mp").astype(jnp.int32)
        ff_cuts = cut_widths(up_weight.shape[1], (9, 9, 6))
        at_cuts = [cut_widths(width, (5, 4, 3)), cut_widths(width, (4, 5, 3))]

        grad_own = cotangent.reshape(-1, width)
        grad_other = swap_mp(grad_own, mp_size)
        media_full = media_feats.reshape(-1, width).astype(F32)
        latents_full = latents.reshape(-1, width).astype(F32)
        media_n, media_hat, media_inv = normalize(media_full, media_gain, media_shift)
        latent_n, latent_hat, latent_inv = normalize(latents_full, latent_gain, latent_shift)
        media_low = media_n.astype(BF16)
        latent_low = latent_n.astype(BF16)
        both_low = jnp.concatenate([media_low, latent_low])
        queries = dot(latent_low, query_weight).astype(BF16)
        key_both = dot(both_low, key_weight).astype(BF16)
        value_both = dot(both_low, value_weight).astype(BF16)
        media_rows = micro * patches

        def keys_of(both, m):
            return jnp.concatenate(
                [
                    both[m * patches : (m + 1) * patches],
                    both[media_rows + m * latent_rows : media_rows + (m + 1) * latent_rows],
                ]
            )

        masks, mixes, norms = [], [], []
        for m in range(micro):
            mask = mask_of(patch_counts[m], patches, latent_rows)
            mixed, log_norm = attend(
                queries[m * latent_rows : (m + 1) * latent_rows],
                keys_of(key_both, m),
                keys_of(value_both, m),
                mask,
                scale,
            )
            masks.append(mask)
            mixes.append(mixed)
            norms.append(log_norm)
        mixed_low = jnp.concatenate(mixes)
        residual = latents_full + dot(mixed_low, out_weight)
        feed_in, feed_hat, feed_inv = normalize(residual, feed_gain, feed_shift)
        feed_own = feed_in.astype(BF16)
        feed_other = swap_mp(feed_own, mp_size)

        feed_all = jnp.concatenate([feed_own, feed_other])
        grad_all = jnp.concatenate([grad_own, grad_other])
        own = feed_own.shape[0]
        up_proj = dot(feed_all, up_weight)
        normal_cdf = 0.5 * (1.0 + lax.erf(up_proj * ROOT_HALF))
        normal_pdf = jnp.exp(-0.5 * up_proj * up_proj) * DENSITY_SCALE
        hidden = (up_proj * normal_cdf).astype(BF16)
        slope = (normal_cdf + up_proj * normal_pdf).astype(BF16)

        grad_down_t = scatter_product(grad_all.T, hidden, ff_cuts, orders, dp_index, False, sizes)

        grad_up = (dot_t(grad_all, down_weight) * slope.astype(F32)).astype(BF16)
        grad_up_w = scatter_product(feed_all.T, grad_up, ff_cuts, orders, dp_index, False, sizes)

        feed_back = dot_t(grad_up, up_weight)
        grad_feed_in = feed_back[:own] + swap_mp(feed_back[own:].astype(BF16), mp_size).astype(F32)
        branch = dot(hidden, down_weight)
        branch_sum = branch[:own] + swap_mp(branch[own:].astype(BF16), mp_size).astype(F32)
        result = (residual + branch_sum).astype(BF16)

        grad_feed_part, grad_feed_gain, grad_feed_shift = normalize_back(
            grad_feed_in, feed_gain, feed_hat, feed_inv
        )
        grad_residual = grad_own.astype(F32) + grad_feed_part
        grad_residual_low = grad_residual.astype(BF16)
        grad_out_t = scatter_product(grad_residual_low.T, mixed_low, at_cuts[0], orders, flat_index, True, sizes)
        grad_mixed = dot_t(grad_residual_low, out_weight).astype(BF16)

        back = [
            attend_back(
                queries[m * latent_rows : (m + 1) * latent_rows],
                keys_of(key_both, m),
                keys_of(value_both, m),
                masks[m],
                scale,
                norms[m],
                grad_mixed[m * latent_rows : (m + 1) * latent_rows],
            )
            for m in range(micro)
        ]
        grad_queries = jnp.concatenate([b[0] for b in back])
        grad_keys = jnp.concatenate([b[1][:patches] for b in back] + [b[1][patches:] for b in back])
        grad_values = jnp.concatenate([b[2][:patches] for b in back] + [b[2][patches:] for b in back])

        both_t = both_low.T
        latent_t = both_t[:, media_rows:]
        grad_key_w = scatter_product(both_t, grad_keys, at_cuts[0], orders, flat_index, True, sizes)
        grad_value_w = scatter_product(both_t, grad_values, at_cuts[1], orders, flat_index, True, sizes)
        grad_query_w = scatter_product(latent_t, grad_queries, at_cuts[1], orders, flat_index, True, sizes)

        grad_both = dot_t(grad_keys, key_weight) + dot_t(grad_values, value_weight)
        grad_latent_n = grad_both[media_rows:] + dot_t(grad_queries, query_weight)
        grad_latent_part, grad_latent_gain, grad_latent_shift = normalize_back(
            grad_latent_n, latent_gain, latent_hat, latent_inv
        )
        grad_media, grad_media_gain, grad_media_shift = normalize_back(
            grad_both[:media_rows], media_gain, media_hat, media_inv
        )
        grad_latents = grad_residual + grad_latent_part
        sums = small_sums(
            [
                grad_media_gain,
                grad_media_shift,
                grad_latent_gain,
                grad_latent_shift,
                grad_feed_gain,
                grad_feed_shift,
            ],
            flat_index,
            orders[0],
            sizes,
        )
        return (
            result.reshape(latents.shape),
            grad_latents.reshape(latents.shape),
            grad_media.reshape(media_feats.shape),
            grad_query_w,
            grad_key_w,
            grad_value_w,
            grad_out_t.T,
            grad_up_w,
            grad_down_t.T,
            *sums,
        )

    return local


def solution(mesh):
    rows = P(None, ("dp", "mp"), None)
    in_specs = (rows, rows, P(None, ("dp", "mp")), rows, P(), P(), P(), P(), P(None, "mp"), P("mp", None)) + (P(),) * 6
    first = P(("dp", "mp"), None)
    out_specs = (rows, rows, rows, first, first, first, P(None, ("dp", "mp")), P("dp", "mp"), P("mp", "dp")) + (
        P(("dp", "mp")),
    ) * 6
    local = build(mesh.shape["dp"], mesh.shape["mp"])
    return jax.shard_map(local, mesh=mesh, in_specs=in_specs, out_specs=out_specs, check_vma=False)
```

time: 1430 us -> 775 us (0.54)
  waiting for transfers between devices: 978 us -> 268 us
  starting transfers between devices: 1.36 us -> 95.5 us
  matrix products: 298 us -> 237 us
  blocking collectives: 41.6 us -> 0 us
  other arithmetic: 40.5 us -> 81.6 us
  local copies, waits for them, and re-layouts: 42.2 us -> 78.6 us
    reduce_scatter x10 -> x0, waiting for transfers between devices: 967 us -> none  [the longest x1 291 us: local(): lax.psum_scatter(term_up, 'dp', scatter_dimension=0, tiled=True)]
    ppermute x0 -> x93, waiting for transfers between devices: none -> 268 us  [the longest x89 268 us: exchange(): lax.ppermute(value, axis, [(i, i ^ flip) for i in range(sizes[axis])])]
    ppermute x0 -> x93, starting transfers between devices: none -> 95.5 us  [the longest x89 94 us: exchange(): lax.ppermute(value, axis, [(i, i ^ flip) for i in range(sizes[axis])])]
    dot_general x58, matrix products: 291 us -> 232 us  [the longest x42 132 us: dot(): return jnp.dot(left, right, preferred_element_type=F32)]
    unnamed x1 -> x0, blocking collectives: 41.6 us -> none
    dynamic_slice x0 -> x74, local copies, waits for them, and re-layouts: none -> 26.7 us  [sided(): lax.dynamic_index_in_dim(parts, side, 1, keepdims=False)]
    convert_element_type x3 -> x58, other arithmetic: 7.33 us -> 27 us  [the longest x54 13.7 us: halving(): sum((t.astype(F32) for t in rear)).astype(rear[0].dtype)]
    transpose x0 -> x6, other arithmetic: none -> 16.2 us  [the longest x1 4.72 us: local(): grad_out_t = scatter_product(grad_residual_low.T, mixed_low, at_cuts[0],...]
  transfers between devices with their start and end apart: 14 -> 93, of which waited for: 7 -> 46; matrix products, arithmetic and copies ran while one was open for 18% -> 37% of each run, Pallas kernels for 0% -> 0%
where the time goes in v1:
time: 775 us; the launch traced here: 764 us
  waiting for transfers between devices  268 us (35%)
  matrix products  237 us (31%)
  starting transfers between devices  95.5 us (12%)
  other arithmetic  81.6 us (11%)
  local copies, waits for them, and re-layouts  78.6 us (10%)
    ppermute x89, waiting for transfers between devices, exchange(): lax.ppermute(value, axis, [(i, i ^ flip) for i in range(sizes[axis])])  268 us
    dot_general x42, matrix products, dot(): return jnp.dot(left, right, preferred_element_type=F32)  132 us
    ppermute x89, starting transfers between devices, exchange(): lax.ppermute(value, axis, [(i, i ^ flip) for i in range(sizes[axis])])  94 us
    dot_general x6, matrix products, dot_t(): return jnp.einsum('rd,ed->re', left, right, preferred_element_type=F32)  53.1 us
    dynamic_slice x74, local copies, waits for them, and re-layouts, sided(): lax.dynamic_index_in_dim(parts, side, 1, keepdims=False)  26.7 us
    dot_general x2, matrix products, attend_back(): jnp.einsum('qhd,khd->hqk', grad_heads, value_heads, preferred_element_typ...  16.3 us
  transfers between devices with their start and end apart: 93, of which 46 were waited for; matrix products, arithmetic and copies ran while one was open for 37% of the time, Pallas kernels for 0%

profile of v1, /device:TPU:0, one launch (start us, length us, event | category | flops | bytes accessed | tf_op | source)
XLA Modules:
  0.0 764.0 jit_solution(1483466971035503007)
XLA Ops:
  27.8 7.8 %convolution_convert_fusion.1 = bf16[1024,1536]{1,0:T(8,128)(2,1)S(1)} fusion(bf16[1536,1536]{1,0:T(8,128)(2,1)} %param.22, bf16[512,1536]{1,0:T(8,128)(2,1)} %copy-done.30, bf16[512,1536]{1,0:T(8,128)(2,1)} %copy-done.31), kind=kOutput, calls=%fused_computation.33 | convolution fusion | flops 4839702528 | bytes 11010048 | tf_op jit(solution)/shard_map/dot_general | solution.py:33
  95.1 17.9 %multiply_convert_fusion.1 = (bf16[1024,3072]{1,0:T(8,128)(2,1)}, f32[1024,3072]{1,0:T(8,128)}) fusion(bf16[1536,3072]{1,0:T(8,128)(2,1)} %param.24, bf16[512,1536]{1,0:T(8,128)(2,1)} %collective-permute-done, bf16[512,1536]{1,0:T(8,128)(2,1)} %add_convert_fusion), kind=kOutput, calls=%fused_computation.7 | convolution fusion | flops 9685696512 | bytes 31457280 | tf_op jit(solution)/shard_map/dot_general | solution.py:33
  113.0 15.3 %multiply_convert_fusion = bf16[1024,3072]{1,0:T(8,128)(2,1)} fusion(bf16[3072,1536]{1,0:T(8,128)(2,1)S(1)} %bitcast.1227, f32[1024,3072]{1,0:T(8,128)} %get-tuple-element.102, bf16[512,1536]{1,0:T(8,128)(2,1)} %collective-permute-done.2, bf16[512,1536]{1,0:T(8,128)(2,1)} %bitcast.15), kind=kOutput, calls=%fused_computation.6 | convolution fusion | flops 9707716608 | bytes 31457280 | tf_op jit(solution)/shard_map/rd,ed->re/dot_general | solution.py:37
  128.3 12.1 %fusion.189 = f32[1024,1536]{1,0:T(8,128)S(1)} fusion(bf16[1024,3072]{1,0:T(8,128)(2,1)} %multiply_convert_fusion, bf16[1536,3072]{1,0:T(8,128)(2,1)S(1)} %bitcast.1225), kind=kOutput, calls=%fused_computation.693 | convolution fusion | flops 9663676416 | bytes 22020096 | tf_op jit(solution)/shard_map/rd,ed->re/dot_general | solution.py:37
  142.4 12.7 %fusion.188 = f32[1024,1536]{1,0:T(8,128)S(1)} fusion(bf16[1024,3072]{1,0:T(8,128)(2,1)} %get-tuple-element.101, bf16[3072,1536]{1,0:T(8,128)(2,1)S(1)} %bitcast.1227), kind=kOutput, calls=%fused_computation.692 | convolution fusion | flops 9663676416 | bytes 22020096 | tf_op jit(solution)/shard_map/dot_general | solution.py:33
  229.4 12.4 %collective-permute-done.72 = bf16[8,96,768]{2,1,0:T(8,128)(2,1)S(1)} collective-permute-done((bf16[8,96,768]{2,1,0:T(8,128)(2,1)S(1)}, bf16[8,96,768]{2,1,0:T(8,128)(2,1)S(1)}, u32[]{:S(2)}, u32[]{:S(2)}) %collective-permute-start.72) | collective-permute-done | bytes 1179680 | tf_op jit(solution)/shard_map/ppermute | solution.py:122
  257.6 7.4 fusion.42
  265.0 7.9 %multiply_reduce_fusion.1 = (f32[16,256]{1,0:T(8,128)S(1)}, f32[16,256,512]{2,1,0:T(8,128)}) fusion(f32[16,256]{1,0:T(8,128)S(1)} %copy-done.88, f32[16,256,512]{2,1,0:T(8,128)} %copy-done.1, pred[256,512]{1,0:T(8,128)(4,1)S(1)} %copy-done.49, bf16[256,16,96]{0,2,1:T(8,128)(2,1)S(1)} %bitcast.1001, bf16[512,16,96]{0,2,1:T(8,128)(2,1)S(1)} %bitcast.891), kind=kOutput, calls=%fused_computation.13 | convolution fusion | flops 415232000 | bytes 19300352 | tf_op jit(solution)/shard_map/qhd,khd->hqk/dot_general | solution.py:81
  274.1 7.3 fusion.39
  281.5 8.4 %multiply_reduce_fusion = (f32[16,256]{1,0:T(8,128)S(1)}, f32[16,256,512]{2,1,0:T(8,128)}) fusion(f32[16,256]{1,0:T(8,128)S(1)} %copy-done.87, f32[16,256,512]{2,1,0:T(8,128)} %copy-done, pred[256,512]{1,0:T(8,128)(4,1)S(1)} %copy-done.47, bf16[256,16,96]{0,2,1:T(8,128)(2,1)S(1)} %bitcast.1003, bf16[512,16,96]{0,2,1:T(8,128)(2,1)S(1)} %bitcast.893), kind=kOutput, calls=%fused_computation.10 | convolution fusion | flops 415232000 | bytes 19300352 | tf_op jit(solution)/shard_map/qhd,khd->hqk/dot_general | solution.py:81
  335.7 7.4 fusion.178
  356.2 8.0 %convolution_add_fusion = f32[1024,1536]{1,0:T(8,128)S(1)} fusion(f32[1024,1536]{1,0:T(8,128)} %fusion.178, bf16[1536,1536]{1,0:T(8,128)(2,1)S(1)} %bitcast.1235, bf16[256,1536]{0,1:T(8,128)(2,1)S(1)} %bitcast.797, bf16[256,1536]{0,1:T(8,128)(2,1)S(1)} %bitcast.791, bf16[256,1536]{0,1:T(8,128)(2,1)S(1)} %bitcast.794, bf16[256,1536]{0,1:T(8,128)(2,1)S(1)} %bitcast.788), kind=kOutput, calls=%fused_computation.25 | convolution fusion | flops 4845993984 | bytes 20447232 | tf_op jit(solution)/shard_map/rd,ed->re/dot_general | solution.py:37
  368.3 7.6 multiply_reduce_fusion.3
  425.0 13.9 %collective-permute-done.85 = bf16[4,96,768]{2,1,0:T(8,128)(2,1)S(1)} collective-permute-done((bf16[4,96,768]{2,1,0:T(8,128)(2,1)S(1)}, bf16[4,96,768]{2,1,0:T(8,128)(2,1)S(1)}, u32[]{:S(2)}, u32[]{:S(2)}) %collective-permute-start.85) | collective-permute-done | bytes 589856 | tf_op jit(solution)/shard_map/ppermute | solution.py:122
  443.5 19.8 %collective-permute-done.73 = bf16[4,96,768]{2,1,0:T(8,128)(2,1)S(1)} collective-permute-done((bf16[4,96,768]{2,1,0:T(8,128)(2,1)S(1)}, bf16[4,96,768]{2,1,0:T(8,128)(2,1)S(1)}, u32[]{:S(2)}, u32[]{:S(2)}) %collective-permute-start.73) | collective-permute-done | bytes 589856 | tf_op jit(solution)/shard_map/ppermute | solution.py:122
  524.3 10.0 %collective-permute-done.61 = bf16[4,48,384]{2,1,0:T(8,128)(2,1)S(1)} collective-permute-done((bf16[4,48,384]{2,1,0:T(8,128)(2,1)S(1)}, bf16[4,48,384]{2,1,0:T(8,128)(2,1)S(1)}, u32[]{:S(2)}, u32[]{:S(2)}) %collective-permute-start.61) | collective-permute-done | bytes 147488 | tf_op jit(solution)/shard_map/ppermute | solution.py:122
  548.9 8.9 %collective-permute-done.65 = bf16[4,96,1152]{2,1,0:T(8,128)(2,1)S(1)} collective-permute-done((bf16[4,96,1152]{2,1,0:T(8,128)(2,1)S(1)}, bf16[4,96,1152]{2,1,0:T(8,128)(2,1)S(1)}, u32[]{:S(2)}, u32[]{:S(2)}) %collective-permute-start.65) | collective-permute-done | bytes 884768 | tf_op jit(solution)/shard_map/ppermute | solution.py:122
  559.5 7.1 collective-permute-done.69
  567.4 14.8 %collective-permute-done.62 = bf16[2,48,384]{2,1,0:T(8,128)(2,1)S(1)} collective-permute-done((bf16[2,48,384]{2,1,0:T(8,128)(2,1)S(1)}, bf16[2,48,384]{2,1,0:T(8,128)(2,1)S(1)}, u32[]{:S(2)}, u32[]{:S(2)}) %collective-permute-start.62) | collective-permute-done | bytes 73760 | tf_op jit(solution)/shard_map/ppermute | solution.py:122
  617.2 13.0 %collective-permute-done.56 = bf16[4,48,512]{2,1,0:T(8,128)(2,1)S(1)} collective-permute-done((bf16[4,48,512]{2,1,0:T(8,128)(2,1)S(1)}, bf16[4,48,512]{2,1,0:T(8,128)(2,1)S(1)}, u32[]{:S(2)}, u32[]{:S(2)}) %collective-permute-start.56) | collective-permute-done | bytes 196640 | tf_op jit(solution)/shard_map/ppermute | solution.py:122
  636.5 7.2 collective-permute-start.78
  652.0 23.9 %collective-permute-done.57 = bf16[2,48,512]{2,1,0:T(8,128)(2,1)S(1)} collective-permute-done((bf16[2,48,512]{2,1,0:T(8,128)(2,1)S(1)}, bf16[2,48,512]{2,1,0:T(8,128)(2,1)S(1)}, u32[]{:S(2)}, u32[]{:S(2)}) %collective-permute-start.57) | collective-permute-done | bytes 98336 | tf_op jit(solution)/shard_map/ppermute | solution.py:122
  698.5 12.5 %collective-permute-done.58 = bf16[1,48,512]{2,1,0:T(8,128)(2,1)S(1)} collective-permute-done((bf16[1,48,512]{2,1,0:T(8,128)(2,1)S(1)}, bf16[1,48,512]{2,1,0:T(8,128)(2,1)S(1)}, u32[]{:S(2)}, u32[]{:S(2)}) %collective-permute-start.58) | collective-permute-done | bytes 49184 | tf_op jit(solution)/shard_map/ppermute | solution.py:122
  734.4 9.4 %collective-permute-done.79 = bf16[1,96,1152]{2,1,0:T(8,128)(2,1)S(1)} collective-permute-done((bf16[1,96,1152]{2,1,0:T(8,128)(2,1)S(1)}, bf16[1,96,1152]{2,1,0:T(8,128)(2,1)S(1)}, u32[]{:S(2)}, u32[]{:S(2)}) %collective-permute-start.79) | collective-permute-done | bytes 221216 | tf_op jit(solution)/shard_map/ppermute | solution.py:122
  (776 shorter events, 487.1 us)
Async XLA Ops:
  141.9 102.3 %collective-permute-start.3 = (bf16[512,1536]{1,0:T(8,128)(2,1)}, bf16[512,1536]{1,0:T(8,128)(2,1)}, u32[]{:S(2)}, u32[]{:S(2)}) collective-permute-start(bf16[512,1536]{1,0:T(8,128)(2,1)} %slice.441), channel_id=1, source_target_pairs={{0,1},{1,0},{2,3},{3,2},{4,5},{5,4},{6,7},{7,6},{8,9},{9,8},{10,11... | collective-permute-start | bytes 4718600 | tf_op jit(solution)/shard_map/ppermute | solution.py:111
  156.6 92.3 %collective-permute-start.1 = (bf16[512,1536]{1,0:T(8,128)(2,1)}, bf16[512,1536]{1,0:T(8,128)(2,1)}, u32[]{:S(2)}, u32[]{:S(2)}) collective-permute-start(bf16[512,1536]{1,0:T(8,128)(2,1)} %slice.442), channel_id=1, source_target_pairs={{0,1},{1,0},{2,3},{3,2},{4,5},{5,4},{6,7},{7,6},{8,9},{9,8},{10,11... | collective-permute-start | bytes 4718600 | tf_op jit(solution)/shard_map/ppermute | solution.py:111
  171.0 245.7 %collective-permute-start.76 = (bf16[8,96,1152]{2,1,0:T(8,128)(2,1)}, bf16[8,96,1152]{2,1,0:T(8,128)(2,1)}, u32[]{:S(2)}, u32[]{:S(2)}) collective-permute-start(bf16[8,96,1152]{2,1,0:T(8,128)(2,1)} %bitcast.300), channel_id=1, source_target_pairs={{0,2},{2,0},{4,6},{6,4},{8,10},{10,8},{12,14},{14,12},{16,18},{18,... | collective-permute-start | bytes 5308424 | tf_op jit(solution)/shard_map/ppermute | solution.py:122
  188.5 35.2 %collective-permute-start.84 = (bf16[8,96,768]{2,1,0:T(8,128)(2,1)}, bf16[8,96,768]{2,1,0:T(8,128)(2,1)}, u32[]{:S(2)}, u32[]{:S(2)}) collective-permute-start(bf16[8,96,768]{2,1,0:T(8,128)(2,1)} %bitcast.330), channel_id=1, source_target_pairs={{0,8},{2,10},{4,12},{6,14},{8,0},{10,2},{12,4},{14,6},{16,24},{18,... | collective-permute-start | bytes 3538952 | tf_op jit(solution)/shard_map/ppermute | solution.py:122
  223.7 196.2 %collective-permute-start.80 = (bf16[8,96,1152]{2,1,0:T(8,128)(2,1)}, bf16[8,96,1152]{2,1,0:T(8,128)(2,1)}, u32[]{:S(2)}, u32[]{:S(2)}) collective-permute-start(bf16[8,96,1152]{2,1,0:T(8,128)(2,1)} %bitcast.315), channel_id=1, source_target_pairs={{0,4},{2,6},{4,0},{6,2},{8,12},{10,14},{12,8},{14,10},{16,20},{18,... | collective-permute-start | bytes 5308424 | tf_op jit(solution)/shard_map/ppermute | solution.py:122
  241.8 181.2 %collective-permute-start.64 = (bf16[8,96,1152]{2,1,0:T(8,128)(2,1)}, bf16[8,96,1152]{2,1,0:T(8,128)(2,1)}, u32[]{:S(2)}, u32[]{:S(2)}) collective-permute-start(bf16[8,96,1152]{2,1,0:T(8,128)(2,1)} %bitcast.254), channel_id=1, source_target_pairs={{0,2},{2,0},{4,6},{6,4},{8,10},{10,8},{12,14},{14,12},{16,18},{18,... | collective-permute-start | bytes 5308424 | tf_op jit(solution)/shard_map/ppermute | solution.py:122
  244.3 196.1 %collective-permute-start.68 = (bf16[8,96,1152]{2,1,0:T(8,128)(2,1)}, bf16[8,96,1152]{2,1,0:T(8,128)(2,1)}, u32[]{:S(2)}, u32[]{:S(2)}) collective-permute-start(bf16[8,96,1152]{2,1,0:T(8,128)(2,1)} %bitcast.269), channel_id=1, source_target_pairs={{0,4},{2,6},{4,0},{6,2},{8,12},{10,14},{12,8},{14,10},{16,20},{18,... | collective-permute-start | bytes 5308424 | tf_op jit(solution)/shard_map/ppermute | solution.py:122
  416.8 46.6 %collective-permute-start.73 = (bf16[4,96,768]{2,1,0:T(8,128)(2,1)S(1)}, bf16[4,96,768]{2,1,0:T(8,128)(2,1)S(1)}, u32[]{:S(2)}, u32[]{:S(2)}) collective-permute-start(bf16[4,96,768]{2,1,0:T(8,128)(2,1)S(1)} %copy-done.79), channel_id=1, source_target_pairs={{0,16},{2,18},{4,20},{6,22},{8,24},{10,26},{12,28},{14,30},{16,0},... | collective-permute-start | bytes 1769480 | tf_op jit(solution)/shard_map/ppermute | solution.py:122
  419.9 98.6 %collective-permute-start.49 = (bf16[16,48,640]{2,1,0:T(8,128)(2,1)S(1)}, bf16[16,48,640]{2,1,0:T(8,128)(2,1)S(1)}, u32[]{:S(2)}, u32[]{:S(2)}) collective-permute-start(bf16[16,48,640]{2,1,0:T(8,128)(2,1)S(1)} %bitcast.1237), channel_id=1, source_target_pairs={{0,1},{1,0},{2,3},{3,2},{4,5},{5,4},{6,7},{7,6},{8,9},{9,8},{10,11... | collective-permute-start | bytes 2949128 | tf_op jit(solution)/shard_map/ppermute | solution.py:122
  423.1 48.7 %collective-permute-start.59 = (bf16[16,48,384]{2,1,0:T(8,128)(2,1)S(1)}, bf16[16,48,384]{2,1,0:T(8,128)(2,1)S(1)}, u32[]{:S(2)}, u32[]{:S(2)}) collective-permute-start(bf16[16,48,384]{2,1,0:T(8,128)(2,1)S(1)} %bitcast.1117), channel_id=1, source_target_pairs={{0,1},{1,0},{2,3},{3,2},{4,5},{5,4},{6,7},{7,6},{8,9},{9,8},{10,11... | collective-permute-start | bytes 1769480 | tf_op jit(solution)/shard_map/ppermute | solution.py:122
  439.0 33.4 %collective-permute-start.44 = (bf16[16,48,384]{2,1,0:T(8,128)(2,1)S(1)}, bf16[16,48,384]{2,1,0:T(8,128)(2,1)S(1)}, u32[]{:S(2)}, u32[]{:S(2)}) collective-permute-start(bf16[16,48,384]{2,1,0:T(8,128)(2,1)S(1)} %bitcast.1243), channel_id=1, source_target_pairs={{0,1},{1,0},{2,3},{3,2},{4,5},{5,4},{6,7},{7,6},{8,9},{9,8},{10,11... | collective-permute-start | bytes 1769480 | tf_op jit(solution)/shard_map/ppermute | solution.py:122
  518.6 39.3 %collective-permute-start.65 = (bf16[4,96,1152]{2,1,0:T(8,128)(2,1)S(1)}, bf16[4,96,1152]{2,1,0:T(8,128)(2,1)S(1)}, u32[]{:S(2)}, u32[]{:S(2)}) collective-permute-start(bf16[4,96,1152]{2,1,0:T(8,128)(2,1)S(1)} %fusion.60), channel_id=1, source_target_pairs={{0,4},{2,6},{4,0},{6,2},{8,12},{10,14},{12,8},{14,10},{16,20},{18,... | collective-permute-start | bytes 2654216 | tf_op jit(solution)/shard_map/ppermute | solution.py:122
  545.8 67.3 %collective-permute-start.55 = (bf16[8,48,512]{2,1,0:T(8,128)(2,1)S(1)}, bf16[8,48,512]{2,1,0:T(8,128)(2,1)S(1)}, u32[]{:S(2)}, u32[]{:S(2)}) collective-permute-start(bf16[8,48,512]{2,1,0:T(8,128)(2,1)S(1)} %bitcast.1137), channel_id=1, source_target_pairs={{0,4},{2,6},{4,0},{6,2},{8,12},{10,14},{12,8},{14,10},{16,20},{18,... | collective-permute-start | bytes 1179656 | tf_op jit(solution)/shard_map/ppermute | solution.py:122
  546.4 65.9 %collective-permute-start.35 = (bf16[8,48,512]{2,1,0:T(8,128)(2,1)S(1)}, bf16[8,48,512]{2,1,0:T(8,128)(2,1)S(1)}, u32[]{:S(2)}, u32[]{:S(2)}) collective-permute-start(bf16[8,48,512]{2,1,0:T(8,128)(2,1)S(1)} %fusion.82), channel_id=1, source_target_pairs={{0,2},{2,0},{4,6},{6,4},{8,10},{10,8},{12,14},{14,12},{16,18},{18,... | collective-permute-start | bytes 1179656 | tf_op jit(solution)/shard_map/ppermute | solution.py:122
  547.2 67.7 %collective-permute-start.25 = (bf16[8,48,512]{2,1,0:T(8,128)(2,1)S(1)}, bf16[8,48,512]{2,1,0:T(8,128)(2,1)S(1)}, u32[]{:S(2)}, u32[]{:S(2)}) collective-permute-start(bf16[8,48,512]{2,1,0:T(8,128)(2,1)S(1)} %bitcast.1138), channel_id=1, source_target_pairs={{0,4},{2,6},{4,0},{6,2},{8,12},{10,14},{12,8},{14,10},{16,20},{18,... | collective-permute-start | bytes 1179656 | tf_op jit(solution)/shard_map/ppermute | solution.py:122
  557.9 57.7 %collective-permute-start.5 = (bf16[8,48,512]{2,1,0:T(8,128)(2,1)S(1)}, bf16[8,48,512]{2,1,0:T(8,128)(2,1)S(1)}, u32[]{:S(2)}, u32[]{:S(2)}) collective-permute-start(bf16[8,48,512]{2,1,0:T(8,128)(2,1)S(1)} %fusion.81), channel_id=1, source_target_pairs={{0,2},{2,0},{4,6},{6,4},{8,10},{10,8},{12,14},{14,12},{16,18},{18,... | collective-permute-start | bytes 1179656 | tf_op jit(solution)/shard_map/ppermute | solution.py:122
  636.5 54.7 %collective-permute-start.78 = (bf16[2,96,1152]{2,1,0:T(8,128)(2,1)S(1)}, bf16[2,96,1152]{2,1,0:T(8,128)(2,1)S(1)}, u32[]{:S(2)}, u32[]{:S(2)}) collective-permute-start(bf16[2,96,1152]{2,1,0:T(8,128)(2,1)S(1)} %fusion.75), channel_id=1, source_target_pairs={{0,8},{2,10},{4,12},{6,14},{8,0},{10,2},{12,4},{14,6},{16,24},{18,... | collective-permute-start | bytes 1327112 | tf_op jit(solution)/shard_map/ppermute | solution.py:122
  643.7 48.3 %collective-permute-start.82 = (bf16[2,96,1152]{2,1,0:T(8,128)(2,1)S(1)}, bf16[2,96,1152]{2,1,0:T(8,128)(2,1)S(1)}, u32[]{:S(2)}, u32[]{:S(2)}) collective-permute-start(bf16[2,96,1152]{2,1,0:T(8,128)(2,1)S(1)} %fusion.76), channel_id=1, source_target_pairs={{0,8},{2,10},{4,12},{6,14},{8,0},{10,2},{12,4},{14,6},{16,24},{18,... | collective-permute-start | bytes 1327112 | tf_op jit(solution)/shard_map/ppermute | solution.py:122
  644.0 48.9 %collective-permute-start.66 = (bf16[2,96,1152]{2,1,0:T(8,128)(2,1)S(1)}, bf16[2,96,1152]{2,1,0:T(8,128)(2,1)S(1)}, u32[]{:S(2)}, u32[]{:S(2)}) collective-permute-start(bf16[2,96,1152]{2,1,0:T(8,128)(2,1)S(1)} %fusion.73), channel_id=1, source_target_pairs={{0,8},{2,10},{4,12},{6,14},{8,0},{10,2},{12,4},{14,6},{16,24},{18,... | collective-permute-start | bytes 1327112 | tf_op jit(solution)/shard_map/ppermute | solution.py:122
  646.2 48.5 %collective-permute-start.70 = (bf16[2,96,1152]{2,1,0:T(8,128)(2,1)S(1)}, bf16[2,96,1152]{2,1,0:T(8,128)(2,1)S(1)}, u32[]{:S(2)}, u32[]{:S(2)}) collective-permute-start(bf16[2,96,1152]{2,1,0:T(8,128)(2,1)S(1)} %fusion.74), channel_id=1, source_target_pairs={{0,8},{2,10},{4,12},{6,14},{8,0},{10,2},{12,4},{14,6},{16,24},{18,... | collective-permute-start | bytes 1327112 | tf_op jit(solution)/shard_map/ppermute | solution.py:122
  689.7 38.3 %collective-permute-start.51 = (bf16[4,48,640]{2,1,0:T(8,128)(2,1)S(1)}, bf16[4,48,640]{2,1,0:T(8,128)(2,1)S(1)}, u32[]{:S(2)}, u32[]{:S(2)}) collective-permute-start(bf16[4,48,640]{2,1,0:T(8,128)(2,1)S(1)} %fusion.92), channel_id=1, source_target_pairs={{0,4},{2,6},{4,0},{6,2},{8,12},{10,14},{12,8},{14,10},{16,20},{18,... | collective-permute-start | bytes 737288 | tf_op jit(solution)/shard_map/ppermute | solution.py:122
  691.2 39.8 %collective-permute-start.41 = (bf16[4,48,640]{2,1,0:T(8,128)(2,1)S(1)}, bf16[4,48,640]{2,1,0:T(8,128)(2,1)S(1)}, u32[]{:S(2)}, u32[]{:S(2)}) collective-permute-start(bf16[4,48,640]{2,1,0:T(8,128)(2,1)S(1)} %fusion.91), channel_id=1, source_target_pairs={{0,2},{2,0},{4,6},{6,4},{8,10},{10,8},{12,14},{14,12},{16,18},{18,... | collective-permute-start | bytes 737288 | tf_op jit(solution)/shard_map/ppermute | solution.py:122
  692.1 39.1 %collective-permute-start.21 = (bf16[4,48,640]{2,1,0:T(8,128)(2,1)S(1)}, bf16[4,48,640]{2,1,0:T(8,128)(2,1)S(1)}, u32[]{:S(2)}, u32[]{:S(2)}) collective-permute-start(bf16[4,48,640]{2,1,0:T(8,128)(2,1)S(1)} %fusion.90), channel_id=1, source_target_pairs={{0,4},{2,6},{4,0},{6,2},{8,12},{10,14},{12,8},{14,10},{16,20},{18,... | collective-permute-start | bytes 737288 | tf_op jit(solution)/shard_map/ppermute | solution.py:122
  692.9 41.4 %collective-permute-start.11 = (bf16[4,48,640]{2,1,0:T(8,128)(2,1)S(1)}, bf16[4,48,640]{2,1,0:T(8,128)(2,1)S(1)}, u32[]{:S(2)}, u32[]{:S(2)}) collective-permute-start(bf16[4,48,640]{2,1,0:T(8,128)(2,1)S(1)} %fusion.89), channel_id=1, source_target_pairs={{0,2},{2,0},{4,6},{6,4},{8,10},{10,8},{12,14},{14,12},{16,18},{18,... | collective-permute-start | bytes 737288 | tf_op jit(solution)/shard_map/ppermute | solution.py:122
  (211 other events, 2359.0 us)

commit v2 on v1

v2 whole, which is shorter than its diff:
```python
import functools

import jax
import jax.numpy as jnp
from jax import lax
from jax.experimental import pallas as pl
from jax.experimental.pallas import tpu as pltpu
from jax.sharding import PartitionSpec as P

HEADS = 16
LAT_IMG = 64
EPSILON = 1e-05
MASKED_SCORE = -1e30
ROOT_HALF = 0.7071067811865476
DENSITY_SCALE = 0.3989422804014327
F32 = jnp.float32
BF16 = jnp.bfloat16
NN = (((1,), (0,)), ((), ()))
NT = (((1,), (1,)), ((), ()))
TN = (((0,), (0,)), ((), ()))
MIB = 1024 * 1024


def mm(left, right, dims=NN):
    return lax.dot_general(left, right, dims, preferred_element_type=F32)


def low_mm(left, right):
    return mm(left, right).astype(BF16)


def normalize(values, gain_vec, shift_vec):
    row_mean = jnp.mean(values, -1, keepdims=True)
    centred = values - row_mean
    inv_scale = lax.rsqrt(jnp.mean(centred * centred, -1, keepdims=True) + EPSILON)
    scaled = centred * inv_scale
    return (scaled * gain_vec + shift_vec, scaled, inv_scale)


def normalize_back(upstream, gain_vec, scaled, inv_scale):
    weighted = upstream * gain_vec
    first_mean = jnp.mean(weighted, -1, keepdims=True)
    second_mean = jnp.mean(weighted * scaled, -1, keepdims=True)
    grad_input = inv_scale * (weighted - first_mean - scaled * second_mean)
    return (grad_input, jnp.sum(upstream * scaled, 0), jnp.sum(upstream, 0))


def mask_biases(counts, step, keys, lats, pair):
    lane = lax.broadcasted_iota(jnp.int32, (1, lats), 1) // LAT_IMG
    first = jnp.zeros((1, lats), jnp.int32)
    past = jnp.zeros((1, lats), jnp.int32)
    total = jnp.int32(0)
    for i in range(counts.shape[1]):
        after = total + counts[step, i]
        first = jnp.where(lane == i, total, first)
        past = jnp.where(lane == i, after, past)
        total = after
    place = lax.broadcasted_iota(jnp.int32, (keys, lats), 0)
    media = jnp.where((place >= first) & (place < past), 0.0, MASKED_SCORE)
    key_image = lax.broadcasted_iota(jnp.int32, (pair, pair), 0) // LAT_IMG
    latent_image = lax.broadcasted_iota(jnp.int32, (pair, pair), 1) // LAT_IMG
    return media, jnp.where(key_image == latent_image, 0.0, MASKED_SCORE)


def spans(total, size):
    return [slice(start, start + size) for start in range(0, total, size)]


def attend_kernel(counts, q, k, v, mixed, norm, *, heads, dim, pair):
    scale = dim**-0.5
    lats = q.shape[0]
    bias_m, bias_l = mask_biases(counts, pl.program_id(0), k.shape[1], lats, pair)
    pairs = spans(lats, pair)
    for j in range(heads):
        c = slice(dim * j, dim * j + dim)
        qh = q[:, c]
        kl = k[1, :, c]
        vl = v[1, :, c]
        s_m = mm(k[0, :, c], qh, NT) * scale + bias_m
        s_l = jnp.concatenate([mm(kl[p], qh[p], NT) * scale + bias_l for p in pairs], 1)
        top = jnp.maximum(jnp.max(s_m, 0, keepdims=True), jnp.max(s_l, 0, keepdims=True))
        e_m = jnp.exp(s_m - top)
        e_l = jnp.exp(s_l - top)
        total = jnp.sum(e_m, 0, keepdims=True) + jnp.sum(e_l, 0, keepdims=True)
        inverse = 1.0 / total
        p_m = (e_m * inverse).astype(BF16)
        p_l = (e_l * inverse).astype(BF16)
        latent_part = jnp.concatenate([mm(p_l[:, p], vl[p], TN) for p in pairs], 0)
        mixed[:, c] = (mm(p_m, v[0, :, c], TN) + latent_part).astype(BF16)
        norm[0, 0, j : j + 1, :] = top + jnp.log(total)


def attend_back_kernel(counts, q, k, v, grad_mixed, norm, grad_q, grad_k, grad_v, *, heads, dim, pair):
    scale = dim**-0.5
    lats = q.shape[0]
    bias_m, bias_l = mask_biases(counts, pl.program_id(0), k.shape[1], lats, pair)
    pairs = spans(lats, pair)
    for j in range(heads):
        c = slice(dim * j, dim * j + dim)
        qh = q[:, c]
        km = k[0, :, c]
        kl = k[1, :, c]
        vl = v[1, :, c]
        gh = grad_mixed[:, c]
        log_norm = norm[0, 0, j : j + 1, :]
        p_m = jnp.exp(mm(km, qh, NT) * scale + bias_m - log_norm)
        s_l = jnp.concatenate([mm(kl[p], qh[p], NT) * scale + bias_l for p in pairs], 1)
        p_l = jnp.exp(s_l - log_norm)
        d_m = mm(v[0, :, c], gh, NT)
        d_l = jnp.concatenate([mm(vl[p], gh[p], NT) for p in pairs], 1)
        row_mean = jnp.sum(d_m * p_m, 0, keepdims=True) + jnp.sum(d_l * p_l, 0, keepdims=True)
        g_m = (p_m * (d_m - row_mean)).astype(BF16)
        g_l = (p_l * (d_l - row_mean)).astype(BF16)
        p_m = p_m.astype(BF16)
        p_l = p_l.astype(BF16)
        grad_v[0, :, c] = mm(p_m, gh).astype(BF16)
        grad_k[0, :, c] = (mm(g_m, qh) * scale).astype(BF16)
        for p in pairs:
            grad_v[1, p, c] = mm(p_l[:, p], gh[p]).astype(BF16)
            grad_k[1, p, c] = (mm(g_l[:, p], qh[p]) * scale).astype(BF16)
        latent_part = jnp.concatenate([mm(g_l[:, p], kl[p], TN) for p in pairs], 0)
        grad_q[:, c] = ((mm(g_m, km, TN) + latent_part) * scale).astype(BF16)


def attention_call(kernel, counts, queries, keys, values, more, outs, flops):
    micro = counts.shape[0]
    rows = queries.shape[0] // micro
    width = queries.shape[1]
    groups = 2
    heads = HEADS // groups
    group = width // groups
    one = pl.BlockSpec((rows, group), lambda m, g: (m, g))
    two = pl.BlockSpec((2, rows, group), lambda m, g: (0, m, g))
    norm = pl.BlockSpec((1, 1, heads, rows), lambda m, g: (m, g, 0, 0))
    kinds = {
        "one": (one, jax.ShapeDtypeStruct(queries.shape, BF16)),
        "two": (two, jax.ShapeDtypeStruct(keys.shape, BF16)),
        "norm": (norm, jax.ShapeDtypeStruct((micro, groups, heads, rows), F32)),
    }
    return pl.pallas_call(
        functools.partial(kernel, heads=heads, dim=width // HEADS, pair=2 * LAT_IMG),
        grid=(micro, groups),
        in_specs=[pl.BlockSpec(memory_space=pltpu.SMEM), one, two, two] + [kinds[kind][0] for kind, _ in more],
        out_specs=[kinds[kind][0] for kind in outs],
        out_shape=[kinds[kind][1] for kind in outs],
        compiler_params=pltpu.CompilerParams(vmem_limit_bytes=40 * MIB),
        cost_estimate=pl.CostEstimate(flops=flops, bytes_accessed=20 * MIB, transcendentals=0),
    )(counts, queries, keys, values, *[value for _, value in more])


def feed_kernel(feed, cot, up, down, *refs, row_step, width_step):
    grad_down, grad_up_w, hidden, grad_up = refs[-4:]
    rows, width = feed.shape
    for r in spans(rows, row_step):
        u = mm(feed[r, :], up[...])
        grad_hidden = mm(cot[r, :], down[...], NT)
        cdf = 0.5 * (1.0 + lax.erf(u * ROOT_HALF))
        pdf = jnp.exp(-0.5 * u * u) * DENSITY_SCALE
        hidden[r, :] = (u * cdf).astype(BF16)
        grad_up[r, :] = (grad_hidden * (cdf + u * pdf)).astype(BF16)
    for r in spans(width, width_step):
        grad_down[r, :] = mm(cot[:, r], hidden[...], TN).astype(BF16)
        grad_up_w[r, :] = mm(feed[:, r], grad_up[...], TN).astype(BF16)


def feed_part(feed, cot, up, down, start, tiles, tile, before):
    rows, width = feed.shape
    whole = pl.BlockSpec((rows, width), lambda t: (0, 0), pipeline_mode=pl.Buffered(1))
    weight_grad = pl.BlockSpec((width, tile), lambda t: (0, t))
    units = pl.BlockSpec((rows, tile), lambda t: (0, start + t))
    unit_shape = jax.ShapeDtypeStruct((rows, up.shape[1]), BF16)
    grad_shape = jax.ShapeDtypeStruct((width, tiles * tile), BF16)
    kept = [] if before is None else list(before)
    return pl.pallas_call(
        functools.partial(feed_kernel, row_step=rows // 2, width_step=width // 2),
        grid=(tiles,),
        in_specs=[
            whole,
            whole,
            pl.BlockSpec((width, tile), lambda t: (0, start + t)),
            pl.BlockSpec((tile, width), lambda t: (start + t, 0)),
        ]
        + [pl.BlockSpec(memory_space=pl.ANY)] * len(kept),
        out_specs=[weight_grad, weight_grad, units, units],
        out_shape=[grad_shape, grad_shape, unit_shape, unit_shape],
        input_output_aliases={4: 2, 5: 3} if kept else {},
        compiler_params=pltpu.CompilerParams(vmem_limit_bytes=60 * MIB),
        cost_estimate=pl.CostEstimate(flops=8 * rows * width * tile * tiles, bytes_accessed=16 * MIB, transcendentals=0),
    )(feed, cot, up, down, *kept)


def product_kernel(left, first, *refs, steps):
    out = refs[-1]
    step = pl.program_id(0)

    @pl.when(step < steps)
    def _():
        out[...] = mm(left[...], first[...], TN).astype(BF16)

    if len(refs) == 2:

        @pl.when(step >= steps)
        def _():
            rows = refs[0].shape[0]
            out[...] = mm(left[left.shape[0] - rows :, :], refs[0][...], TN).astype(BF16)


def product(left, first, second=None, part=0):
    rows, width = left.shape
    tile = width // 2
    steps = first.shape[1] // tile
    grid = steps + (second is not None)
    in_specs = [
        pl.BlockSpec((rows, width), lambda t: (0, 0), pipeline_mode=pl.Buffered(1)),
        pl.BlockSpec((rows, tile), lambda t: (0, jnp.minimum(t, steps - 1))),
    ]
    operands = [left, first]
    if second is not None:
        in_specs.append(pl.BlockSpec((second.shape[0], tile), lambda t: (0, part)))
        operands.append(second)
    return pl.pallas_call(
        functools.partial(product_kernel, steps=steps),
        grid=(grid,),
        in_specs=in_specs,
        out_specs=pl.BlockSpec((width, tile), lambda t: (0, t)),
        out_shape=jax.ShapeDtypeStruct((width, grid * tile), BF16),
        compiler_params=pltpu.CompilerParams(vmem_limit_bytes=40 * MIB),
        cost_estimate=pl.CostEstimate(flops=2 * rows * width * tile * grid, bytes_accessed=12 * MIB, transcendentals=0),
    )(*operands)


def bit_orders(count):
    bits = count.bit_length() - 1
    if bits == 4:
        return [(0, 1, 2, 3), (1, 0, 2, 3), (2, 3, 0, 1)]
    plain = tuple(range(bits))
    third = bits // 3
    return [plain[s:] + plain[:s] for s in (0, third, 2 * third)]


def sided(value, bit, bits, side):
    place = bits.index(bit)
    shape = value.shape
    outer = 1 << place
    parts = value.reshape((outer, 2, shape[0] // (2 * outer)) + shape[1:])
    return lax.dynamic_index_in_dim(parts, side, 1, keepdims=False).reshape((shape[0] // 2,) + shape[1:])


def swap_mp(value, size):
    return lax.ppermute(value, "mp", [(i, i ^ 1) for i in range(size)])


def steps_of(order, with_mp):
    if with_mp:
        return [("mp", 0)] + [("dp", bit + 1) for bit in order]
    return [("dp", bit) for bit in order]


def exchange(value, axis, bit, shifted, sizes):
    flip = 1 if axis == "mp" else 1 << (bit - shifted)
    return lax.ppermute(value, axis, [(i, i ^ flip) for i in range(sizes[axis])])


def halving(terms, bits, steps, block_index, shifted, sizes):
    for axis, bit in steps:
        mine = (block_index >> bit) & 1
        rear = [sided(t, bit, bits, 1 - mine) for t in terms]
        sent = rear[0] if len(rear) == 1 else sum(t.astype(F32) for t in rear).astype(rear[0].dtype)
        got = exchange(sent, axis, bit, shifted, sizes)
        terms = [sided(t, bit, bits, mine) for t in terms] + [got]
        bits = [b for b in bits if b != bit]
    return sum(t[0].astype(F32) for t in terms)


def scatter_partials(partials, order, block_index, with_mp, sizes):
    blocks = sizes["dp"] * (sizes["mp"] if with_mp else 1)
    width = partials.shape[0]
    all_bits = list(range(blocks.bit_length() - 1))[::-1]
    parted = partials.reshape(blocks, width // blocks, -1)
    return halving([parted], all_bits, steps_of(order, with_mp), block_index, 1 if with_mp else 0, sizes)


def small_sums(vectors, block_index, order, sizes):
    blocks = sizes["dp"] * sizes["mp"]
    count = len(vectors)
    stacked = jnp.stack(vectors).reshape(count, blocks, -1).transpose(1, 0, 2)
    all_bits = list(range(blocks.bit_length() - 1))[::-1]
    share = halving([stacked], all_bits, steps_of(order, True), block_index, 1, sizes)
    return [share[i] for i in range(count)]


def build(dp_size, mp_size):
    plain, swapped, last = bit_orders(dp_size)
    sizes = {"dp": dp_size, "mp": mp_size}

    def swap(value):
        return lax.ppermute(value, "mp", [(i, i ^ 1) for i in range(mp_size)])

    def local(
        media_feats,
        latents,
        patch_counts,
        cotangent,
        query_weight,
        key_weight,
        value_weight,
        out_weight,
        up_weight,
        down_weight,
        media_gain,
        media_shift,
        latent_gain,
        latent_shift,
        feed_gain,
        feed_shift,
    ):
        micro, patches, width = media_feats.shape
        dp_index = lax.axis_index("dp").astype(jnp.int32)
        flat_index = dp_index * mp_size + lax.axis_index("mp").astype(jnp.int32)

        grad_own = cotangent.reshape(-1, width)
        grad_all = jnp.concatenate([grad_own, swap(grad_own)])
        media_full = media_feats.reshape(-1, width).astype(F32)
        latents_full = latents.reshape(-1, width).astype(F32)
        media_n, media_hat, media_inv = normalize(media_full, media_gain, media_shift)
        latent_n, latent_hat, latent_inv = normalize(latents_full, latent_gain, latent_shift)
        latent_low = latent_n.astype(BF16)
        both_low = jnp.concatenate([media_n.astype(BF16), latent_low])
        queries = low_mm(latent_low, query_weight)
        keys = low_mm(both_low, key_weight).reshape(2, -1, width)
        values = low_mm(both_low, value_weight).reshape(2, -1, width)
        own = latent_low.shape[0]
        work = 4 * own * (patches + 2 * LAT_IMG) * width
        mixed_low, log_norm = attention_call(
            attend_kernel, patch_counts, queries, keys, values, [], ["one", "norm"], work
        )
        residual = latents_full + mm(mixed_low, out_weight)
        feed_in, feed_hat, feed_inv = normalize(residual, feed_gain, feed_shift)
        feed_own = feed_in.astype(BF16)
        feed_all = jnp.concatenate([feed_own, swap(feed_own)])

        tile = 512
        tiles = up_weight.shape[1] // tile
        second = tiles // 3
        third = tiles // 6
        shares = [(tiles - second - third, plain, swapped), (second, swapped, plain), (third, last, last)]
        before = None
        start = 0
        down_pieces, up_pieces = [], []
        for count, down_order, up_order in shares:
            grad_down, grad_up_w, *before = feed_part(
                feed_all, grad_all, up_weight, down_weight, start, count, tile, before
            )
            start += count
            if down_order is up_order:
                joined = jnp.concatenate([grad_down, grad_up_w], 1)
                piece = scatter_partials(joined, down_order, dp_index, False, sizes)
                half = piece.shape[1] // 2
                down_pieces.append(piece[:, :half])
                up_pieces.append(piece[:, half:])
            else:
                down_pieces.append(scatter_partials(grad_down, down_order, dp_index, False, sizes))
                up_pieces.append(scatter_partials(grad_up_w, up_order, dp_index, False, sizes))
        hidden, grad_up = before

        feed_back_other = mm(grad_up[own:], up_weight, NT).astype(BF16)
        grad_feed_in = mm(grad_up[:own], up_weight, NT) + swap(feed_back_other).astype(F32)
        grad_feed_part, grad_feed_gain, grad_feed_shift = normalize_back(
            grad_feed_in, feed_gain, feed_hat, feed_inv
        )
        grad_residual = grad_own.astype(F32) + grad_feed_part
        grad_residual_low = grad_residual.astype(BF16)
        grad_out_t = scatter_partials(product(grad_residual_low, mixed_low), last, flat_index, True, sizes)
        grad_mixed = mm(grad_residual_low, out_weight, NT).astype(BF16)

        grad_queries, grad_keys, grad_values = attention_call(
            attend_back_kernel,
            patch_counts,
            queries,
            keys,
            values,
            [("one", grad_mixed), ("norm", log_norm)],
            ["one", "two", "two"],
            2 * work,
        )
        grad_keys = grad_keys.reshape(-1, width)
        grad_values = grad_values.reshape(-1, width)
        key_sums = scatter_partials(product(both_low, grad_keys, grad_queries, 0), plain, flat_index, True, sizes)
        value_sums = scatter_partials(
            product(both_low, grad_values, grad_queries, 1), swapped, flat_index, True, sizes
        )
        grad_query_w = jnp.concatenate([key_sums[:, width:], value_sums[:, width:]], 1)

        grad_both = mm(grad_keys, key_weight, NT) + mm(grad_values, value_weight, NT)
        media_rows = micro * patches
        grad_latent_n = grad_both[media_rows:] + mm(grad_queries, query_weight, NT)
        grad_latent_part, grad_latent_gain, grad_latent_shift = normalize_back(
            grad_latent_n, latent_gain, latent_hat, latent_inv
        )
        grad_media, grad_media_gain, grad_media_shift = normalize_back(
            grad_both[:media_rows], media_gain, media_hat, media_inv
        )
        grad_latents = grad_residual + grad_latent_part
        branch_other = mm(hidden[own:], down_weight).astype(BF16)
        branch = mm(hidden[:own], down_weight) + swap(branch_other).astype(F32)
        result = (residual + branch).astype(BF16)
        sums = small_sums(
            [
                grad_media_gain,
                grad_media_shift,
                grad_latent_gain,
                grad_latent_shift,
                grad_feed_gain,
                grad_feed_shift,
            ],
            flat_index,
            plain,
            sizes,
        )
        return (
            result.reshape(latents.shape),
            grad_latents.reshape(latents.shape),
            grad_media.reshape(media_feats.shape),
            grad_query_w,
            key_sums[:, :width],
            value_sums[:, :width],
            grad_out_t.T,
            jnp.concatenate(up_pieces, 1),
            jnp.concatenate(down_pieces, 1).T,
            *sums,
        )

    return local


def solution(mesh):
    rows = P(None, ("dp", "mp"), None)
    in_specs = (rows, rows, P(None, ("dp", "mp")), rows, P(), P(), P(), P(), P(None, "mp"), P("mp", None)) + (P(),) * 6
    first = P(("dp", "mp"), None)
    out_specs = (rows, rows, rows, first, first, first, P(None, ("dp", "mp")), P("dp", "mp"), P("mp", "dp")) + (
        P(("dp", "mp")),
    ) * 6
    local = build(mesh.shape["dp"], mesh.shape["mp"])
    return jax.shard_map(local, mesh=mesh, in_specs=in_specs, out_specs=out_specs, check_vma=False)
```

time: 775 us -> 587 us (0.76)
  matrix products: 237 us -> 85.4 us
  Pallas kernels: 0 us -> 111 us
  starting transfers between devices: 95.5 us -> 32.6 us
  waiting for transfers between devices: 268 us -> 235 us
  local copies, waits for them, and re-layouts: 78.6 us -> 51.9 us
  other arithmetic: 81.6 us -> 59.2 us
    dot_general x60 -> x12, matrix products: 237 us -> 85.4 us  [mm(): return lax.dot_general(left, right, dims, preferred_element_type=F32)]
    pallas_call x0 -> x8, Pallas kernels: none -> 111 us  [the longest x3 56.4 us: feed_part(): pl.pallas_call(functools.partial(feed_kernel, row_step=rows // 2, width_s...]
    ppermute x89 -> x40, starting transfers between devices: 94 us -> 32 us  [exchange(): lax.ppermute(value, axis, [(i, i ^ flip) for i in range(sizes[axis])])]
    ppermute x89 -> x40, waiting for transfers between devices: 268 us -> 235 us  [exchange(): lax.ppermute(value, axis, [(i, i ^ flip) for i in range(sizes[axis])])]
    slice x16 -> x5, local copies, waits for them, and re-layouts: 18.7 us -> 1.52 us  [the longest x1 0.73 us: local(): key_sums[:, :width]]
    dynamic_slice x74 -> x38, local copies, waits for them, and re-layouts: 26.7 us -> 41.4 us  [sided(): lax.dynamic_index_in_dim(parts, side, 1, keepdims=False)]
    transpose x4 -> x1, other arithmetic: 14.3 us -> 1.1 us  [local(): jnp.concatenate(down_pieces, 1)]
    transpose x4 -> x0, local copies, waits for them, and re-layouts: 11.4 us -> none  [the longest x1 3.58 us: local(): grad_up_w = scatter_product(feed_all.T, grad_up, ff_cuts, orders, dp_inde...]
  transfers between devices with their start and end apart: 93 -> 44, of which waited for: 46 -> 24; matrix products, arithmetic and copies ran while one was open for 37% -> 30% of each run, Pallas kernels for 0% -> 11%
where the time goes in v2:
time: 587 us; the launch traced here: 578 us
  waiting for transfers between devices  235 us (40%)
  Pallas kernels  111 us (19%)
  matrix products  85.4 us (15%)
  other arithmetic  59.2 us (10%)
  local copies, waits for them, and re-layouts  51.9 us (9%)
  starting transfers between devices  32.6 us (6%)
    ppermute x40, waiting for transfers between devices, exchange(): lax.ppermute(value, axis, [(i, i ^ flip) for i in range(sizes[axis])])  235 us
    dot_general x12, matrix products, mm(): return lax.dot_general(left, right, dims, preferred_element_type=F32)  85.4 us
    pallas_call x3, Pallas kernels, feed_part(): pl.pallas_call(functools.partial(feed_kernel, row_step=rows // 2, width_s...  56.4 us
    dynamic_slice x38, local copies, waits for them, and re-layouts, sided(): lax.dynamic_index_in_dim(parts, side, 1, keepdims=False)  41.4 us
    pallas_call x2, Pallas kernels, attention_call(): pl.pallas_call(functools.partial(kernel, heads=heads, dim=width // HEADS,...  32.9 us
    ppermute x40, starting transfers between devices, exchange(): lax.ppermute(value, axis, [(i, i ^ flip) for i in range(sizes[axis])])  32 us
    pallas_call x3, Pallas kernels, product(): pl.pallas_call(functools.partial(product_kernel, steps=steps), grid=(grid...  21.3 us
    convert_element_type x24, other arithmetic, halving(): sum((t.astype(F32) for t in rear)).astype(rear[0].dtype)  16.8 us
  transfers between devices with their start and end apart: 44, of which 24 were waited for; matrix products, arithmetic and copies ran while one was open for 30% of the time, Pallas kernels for 11%

profile of v2, /device:TPU:0, one launch (start us, length us, event | category | flops | bytes accessed | tf_op | source)
XLA Modules:
  0.0 577.7 jit_solution(12927621498402428889)
XLA Ops:
  22.9 15.4 %shard_map.271 = (bf16[512,1536]{1,0:T(8,128)(2,1)S(1)}, f32[2,2,8,256]{3,2,1,0:T(8,128)S(1)}) custom-call(s32[2,4]{1,0:T(2,128)S(1)} %copy-done.5, bf16[512,1536]{1,0:T(8,128)(2,1)S(1)} %convolution_convert_fusion.3.q, bf16[2,512,1536]{2,1,0:T(8,128)(2,1)S(1)} %bitcast.340, bf16[2,512,1536]{2,1,0:T(8,128)(2,1)S(1)} %bitcast.342), custom_call_target="tpu_custom_call" | custom-call | flops 1207959552 | bytes 20971520 | tf_op jit(solution)/shard_map/pallas_call | solution.py:140
  54.4 25.5 %shard_map.272 = (bf16[1536,1536]{1,0:T(8,128)(2,1)}, bf16[1536,1536]{1,0:T(8,128)(2,1)}, bf16[1024,3072]{1,0:T(8,128)(2,1)}, bf16[1024,3072]{1,0:T(8,128)(2,1)}) custom-call(bf16[1024,1536]{1,0:T(8,128)(2,1)} %pad_maximum_fusion.1.feed, bf16[1024,1536]{1,0:T(8,128)(2,1)} %pad_maximum_fusion.2.cot, bf16[1536,3072]{1,0:T(8,128)(2,1)} %up.5, ...), custom_call_target="tpu_custom_call" | custom-call | flops 19327352832 | bytes 16777216 | tf_op jit(solution)/shard_map/pallas_call | solution.py:174
  85.5 18.9 %shard_map.273 = (bf16[1536,1024]{1,0:T(8,128)(2,1)}, bf16[1536,1024]{1,0:T(8,128)(2,1)}, bf16[1024,3072]{1,0:T(8,128)(2,1)}, bf16[1024,3072]{1,0:T(8,128)(2,1)}) custom-call(bf16[1024,1536]{1,0:T(8,128)(2,1)} %pad_maximum_fusion.1.feed, bf16[1024,1536]{1,0:T(8,128)(2,1)} %pad_maximum_fusion.2.cot, ...), custom_call_target="tpu_custom_call", output_to_operand_aliasing={{2}: (4, {}), {3}: (5, {})} | custom-call | flops 12884901888 | bytes 16777216 | tf_op jit(solution)/shard_map/pallas_call | solution.py:174
  118.5 12.0 %shard_map.274 = (bf16[1536,512]{1,0:T(8,128)(2,1)}, bf16[1536,512]{1,0:T(8,128)(2,1)}, bf16[1024,3072]{1,0:T(8,128)(2,1)}, bf16[1024,3072]{1,0:T(8,128)(2,1)}) custom-call(bf16[1024,1536]{1,0:T(8,128)(2,1)} %pad_maximum_fusion.1.feed, bf16[1024,1536]{1,0:T(8,128)(2,1)} %pad_maximum_fusion.2.cot, ...), custom_call_target="tpu_custom_call", output_to_operand_aliasing={{2}: (4, {}), {3}: (5, {})} | custom-call | flops 6442450944 | bytes 16777216 | tf_op jit(solution)/shard_map/pallas_call | solution.py:174
  130.5 10.7 %fusion.15 = bf16[512,1536]{1,0:T(8,128)(2,1)} fusion(bf16[1536,3072]{1,0:T(8,128)(2,1)} %up.5, bf16[1024,3072]{1,0:T(8,128)(2,1)} %get-tuple-element.38), kind=kOutput, calls=%fused_computation.45 | convolution fusion | flops 4832624640 | bytes 14155776 | tf_op jit(solution)/shard_map/dot_general | solution.py:25
  159.1 10.8 %multiply_reduce_fusion = (f32[1536]{0:T(1024)S(1)}, f32[512]{0:T(512)S(1)}, f32[512]{0:T(512)S(1)}, f32[1536]{0:T(1024)S(1)}, f32[512,1536]{1,0:T(8,128)S(1)}) fusion(f32[512,1536]{1,0:T(8,128)S(1)} %copy-done.11, f32[512]{0:T(512)S(1)} %add_rsqrt_fusion, f32[512]{0:T(512)S(1)} %broadcast_multiply_fusion.6, f32[1536]{0:T(1024)S(1)} %copy-done.37, ...), kind=kOutput, calls=%fused_computation.17 | convolution fusion | flops 4840484864 | bytes 20473856 | tf_op jit(solution)/shard_map/dot_general | solution.py:25
  183.5 14.1 %collective-permute-done.35 = bf16[8,96,1024]{2,1,0:T(8,128)(2,1)} collective-permute-done((bf16[8,96,1024]{2,1,0:T(8,128)(2,1)}, bf16[8,96,1024]{2,1,0:T(8,128)(2,1)}, u32[]{:S(2)}, u32[]{:S(2)}) %collective-permute-start.35) | collective-permute-done | bytes 1572896 | tf_op jit(solution)/shard_map/ppermute | solution.py:261
  204.1 17.5 %shard_map.275 = (bf16[512,1536]{1,0:T(8,128)(2,1)S(1)}, bf16[2,512,1536]{2,1,0:T(8,128)(2,1)S(1)}, bf16[2,512,1536]{2,1,0:T(8,128)(2,1)S(1)}) custom-call(s32[2,4]{1,0:T(2,128)S(1)} %copy-done.5, bf16[512,1536]{1,0:T(8,128)(2,1)S(1)} %copy-done.2, bf16[2,512,1536]{2,1,0:T(8,128)(2,1)S(1)} %bitcast.341, bf16[2,512,1536]{2,1,0:T(8,128)(2,1)} %bitcast.343, ...), custom_call_target="tpu_custom_call" | custom-call | flops 2415919104 | bytes 20971520 | tf_op jit(solution)/shard_map/pallas_call | solution.py:140
  221.6 9.3 %fusion.63 = f32[1024,1536]{1,0:T(8,128)} fusion(bf16[1024,1536]{1,0:T(8,128)(2,1)S(1)} %bitcast.345, bf16[1536,1536]{1,0:T(8,128)(2,1)} %param.21), kind=kOutput, calls=%fused_computation.226 | convolution fusion | flops 4831838208 | bytes 14155776 | tf_op jit(solution)/shard_map/dot_general | solution.py:25
  230.9 8.7 %convolution_add_fusion = f32[1024,1536]{1,0:T(8,128)S(1)} fusion(f32[1024,1536]{1,0:T(8,128)} %fusion.63, bf16[1024,1536]{1,0:T(8,128)(2,1)S(1)} %bitcast.347, bf16[1536,1536]{1,0:T(8,128)(2,1)} %param.22), kind=kOutput, calls=%fused_computation | convolution fusion | flops 4833411072 | bytes 20447232 | tf_op jit(solution)/shard_map/dot_general | solution.py:25
  243.8 8.7 %shard_map.277 = bf16[1536,2304]{1,0:T(8,128)(2,1)} custom-call(bf16[1024,1536]{1,0:T(8,128)(2,1)S(1)} %copy-done.4, bf16[1024,1536]{1,0:T(8,128)(2,1)S(1)} %bitcast.348, bf16[512,1536]{1,0:T(8,128)(2,1)S(1)} %get-tuple-element.42.refs_0_), custom_call_target="tpu_custom_call" | custom-call | flops 7247757312 | bytes 12582912 | tf_op jit(solution)/shard_map/pallas_call | solution.py:221
  252.6 8.8 %shard_map.276 = bf16[1536,2304]{1,0:T(8,128)(2,1)} custom-call(bf16[1024,1536]{1,0:T(8,128)(2,1)S(1)} %copy-done.4, bf16[1024,1536]{1,0:T(8,128)(2,1)S(1)} %bitcast.346, bf16[512,1536]{1,0:T(8,128)(2,1)S(1)} %get-tuple-element.42.refs_0_), custom_call_target="tpu_custom_call" | custom-call | flops 7247757312 | bytes 12582912 | tf_op jit(solution)/shard_map/pallas_call | solution.py:221
  296.3 10.3 %add_convert_fusion.2 = bf16[512,1536]{1,0:T(8,128)(2,1)} fusion(f32[512,1536]{1,0:T(8,128)S(1)} %copy-done.12, bf16[512,1536]{1,0:T(8,128)(2,1)} %collective-permute-done.2, bf16[3072,1536]{1,0:T(8,128)(2,1)} %down.5, bf16[1024,3072]{1,0:T(8,128)(2,1)S(1)} %bitcast.376), kind=kOutput, calls=%fused_computation.31 | convolution fusion | flops 4834983936 | bytes 18874368 | tf_op jit(solution)/shard_map/dot_general | solution.py:25
  323.7 18.3 %collective-permute-done.43 = f32[1,6,48]{2,0,1:T(1,128)S(1)} collective-permute-done((f32[1,6,48]{2,0,1:T(1,128)S(1)}, f32[1,6,48]{2,0,1:T(1,128)S(1)}, u32[]{:S(2)}, u32[]{:S(2)}) %collective-permute-start.43) | collective-permute-done | bytes 1184 | tf_op jit(solution)/shard_map/ppermute | solution.py:261
  347.9 10.9 %collective-permute-done.28 = bf16[4,96,1024]{2,1,0:T(8,128)(2,1)S(1)} collective-permute-done((bf16[4,96,1024]{2,1,0:T(8,128)(2,1)S(1)}, bf16[4,96,1024]{2,1,0:T(8,128)(2,1)S(1)}, u32[]{:S(2)}, u32[]{:S(2)}) %collective-permute-start.28) | collective-permute-done | bytes 786464 | tf_op jit(solution)/shard_map/ppermute | solution.py:261
  392.2 11.5 %collective-permute-done.26 = bf16[1,96,1024]{2,1,0:T(8,128)(2,1)S(1)} collective-permute-done((bf16[1,96,1024]{2,1,0:T(8,128)(2,1)S(1)}, bf16[1,96,1024]{2,1,0:T(8,128)(2,1)S(1)}, u32[]{:S(2)}, u32[]{:S(2)}) %collective-permute-start.26) | collective-permute-done | bytes 196640 | tf_op jit(solution)/shard_map/ppermute | solution.py:261
  407.7 12.1 %collective-permute-done.33 = bf16[2,96,1536]{2,1,0:T(8,128)(2,1)S(1)} collective-permute-done((bf16[2,96,1536]{2,1,0:T(8,128)(2,1)S(1)}, bf16[2,96,1536]{2,1,0:T(8,128)(2,1)S(1)}, u32[]{:S(2)}, u32[]{:S(2)}) %collective-permute-start.33) | collective-permute-done | bytes 589856 | tf_op jit(solution)/shard_map/ppermute | solution.py:261
  422.6 16.2 %collective-permute-done.21 = bf16[2,96,1536]{2,1,0:T(8,128)(2,1)S(1)} collective-permute-done((bf16[2,96,1536]{2,1,0:T(8,128)(2,1)S(1)}, bf16[2,96,1536]{2,1,0:T(8,128)(2,1)S(1)}, u32[]{:S(2)}, u32[]{:S(2)}) %collective-permute-start.21) | collective-permute-done | bytes 589856 | tf_op jit(solution)/shard_map/ppermute | solution.py:261
  440.4 27.0 %collective-permute-done.22 = bf16[1,96,1536]{2,1,0:T(8,128)(2,1)S(1)} collective-permute-done((bf16[1,96,1536]{2,1,0:T(8,128)(2,1)S(1)}, bf16[1,96,1536]{2,1,0:T(8,128)(2,1)S(1)}, u32[]{:S(2)}, u32[]{:S(2)}) %collective-permute-start.22) | collective-permute-done | bytes 294944 | tf_op jit(solution)/shard_map/ppermute | solution.py:261
  474.9 23.0 %collective-permute-done.16 = bf16[4,48,1536]{2,1,0:T(8,128)(2,1)S(1)} collective-permute-done((bf16[4,48,1536]{2,1,0:T(8,128)(2,1)S(1)}, bf16[4,48,1536]{2,1,0:T(8,128)(2,1)S(1)}, u32[]{:S(2)}, u32[]{:S(2)}) %collective-permute-start.16) | collective-permute-done | bytes 589856 | tf_op jit(solution)/shard_map/ppermute | solution.py:261
  498.8 20.9 %collective-permute-done.17 = bf16[2,48,1536]{2,1,0:T(8,128)(2,1)S(1)} collective-permute-done((bf16[2,48,1536]{2,1,0:T(8,128)(2,1)S(1)}, bf16[2,48,1536]{2,1,0:T(8,128)(2,1)S(1)}, u32[]{:S(2)}, u32[]{:S(2)}) %collective-permute-start.17) | collective-permute-done | bytes 294944 | tf_op jit(solution)/shard_map/ppermute | solution.py:261
  523.7 17.5 %collective-permute-done.11 = bf16[4,48,2304]{2,1,0:T(8,128)(2,1)S(1)} collective-permute-done((bf16[4,48,2304]{2,1,0:T(8,128)(2,1)S(1)}, bf16[4,48,2304]{2,1,0:T(8,128)(2,1)S(1)}, u32[]{:S(2)}, u32[]{:S(2)}) %collective-permute-start.11) | collective-permute-done | bytes 884768 | tf_op jit(solution)/shard_map/ppermute | solution.py:261
  544.6 12.3 %collective-permute-done.12 = bf16[2,48,2304]{2,1,0:T(8,128)(2,1)S(1)} collective-permute-done((bf16[2,48,2304]{2,1,0:T(8,128)(2,1)S(1)}, bf16[2,48,2304]{2,1,0:T(8,128)(2,1)S(1)}, u32[]{:S(2)}, u32[]{:S(2)}) %collective-permute-start.12) | collective-permute-done | bytes 442400 | tf_op jit(solution)/shard_map/ppermute | solution.py:261
  564.3 8.8 %collective-permute-done.13 = bf16[1,48,2304]{2,1,0:T(8,128)(2,1)S(1)} collective-permute-done((bf16[1,48,2304]{2,1,0:T(8,128)(2,1)S(1)}, bf16[1,48,2304]{2,1,0:T(8,128)(2,1)S(1)}, u32[]{:S(2)}, u32[]{:S(2)}) %collective-permute-start.13) | collective-permute-done | bytes 221216 | tf_op jit(solution)/shard_map/ppermute | solution.py:261
  (357 shorter events, 226.0 us)
Async XLA Ops:
  0.7 46.7 %collective-permute-start.1 = (bf16[512,1536]{1,0:T(8,128)(2,1)}, bf16[512,1536]{1,0:T(8,128)(2,1)}, u32[]{:S(2)}, u32[]{:S(2)}) collective-permute-start(bf16[512,1536]{1,0:T(8,128)(2,1)} %bitcast.377), channel_id=1, source_target_pairs={{0,1},{1,0},{2,3},{3,2},{4,5},{5,4},{6,7},{7,6},{8,9},{9,8},{10,11... | collective-permute-start | bytes 4718600 | tf_op jit(solution)/shard_map/ppermute | solution.py:297
  109.2 235.1 %collective-permute-start.19 = (bf16[8,96,1536]{2,1,0:T(8,128)(2,1)}, bf16[8,96,1536]{2,1,0:T(8,128)(2,1)}, u32[]{:S(2)}, u32[]{:S(2)}) collective-permute-start(bf16[8,96,1536]{2,1,0:T(8,128)(2,1)} %bitcast.70), channel_id=1, source_target_pairs={{0,4},{2,6},{4,0},{6,2},{8,12},{10,14},{12,8},{14,10},{16,20},{18,... | collective-permute-start | bytes 7077896 | tf_op jit(solution)/shard_map/ppermute | solution.py:261
  117.1 225.5 %collective-permute-start.31 = (bf16[8,96,1536]{2,1,0:T(8,128)(2,1)}, bf16[8,96,1536]{2,1,0:T(8,128)(2,1)}, u32[]{:S(2)}, u32[]{:S(2)}) collective-permute-start(bf16[8,96,1536]{2,1,0:T(8,128)(2,1)} %get-tuple-element.68), channel_id=1, source_target_pairs={{0,2},{2,0},{4,6},{6,4},{8,10},{10,8},{12,14},{14,12},{16,18},{18,... | collective-permute-start | bytes 7077896 | tf_op jit(solution)/shard_map/ppermute | solution.py:261
  141.2 56.3 %collective-permute-start.35 = (bf16[8,96,1024]{2,1,0:T(8,128)(2,1)}, bf16[8,96,1024]{2,1,0:T(8,128)(2,1)}, u32[]{:S(2)}, u32[]{:S(2)}) collective-permute-start(bf16[8,96,1024]{2,1,0:T(8,128)(2,1)} %bitcast.126), channel_id=1, source_target_pairs={{0,4},{2,6},{4,0},{6,2},{8,12},{10,14},{12,8},{14,10},{16,20},{18,... | collective-permute-start | bytes 4718600 | tf_op jit(solution)/shard_map/ppermute | solution.py:261
  144.1 124.4 %collective-permute-start.23 = (bf16[8,96,1024]{2,1,0:T(8,128)(2,1)}, bf16[8,96,1024]{2,1,0:T(8,128)(2,1)}, u32[]{:S(2)}, u32[]{:S(2)}) collective-permute-start(bf16[8,96,1024]{2,1,0:T(8,128)(2,1)} %get-tuple-element.72), channel_id=1, source_target_pairs={{0,2},{2,0},{4,6},{6,4},{8,10},{10,8},{12,14},{14,12},{16,18},{18,... | collective-permute-start | bytes 4718600 | tf_op jit(solution)/shard_map/ppermute | solution.py:261
  159.1 135.7 %collective-permute-start.2 = (bf16[512,1536]{1,0:T(8,128)(2,1)}, bf16[512,1536]{1,0:T(8,128)(2,1)}, u32[]{:S(2)}, u32[]{:S(2)}) collective-permute-start(bf16[512,1536]{1,0:T(8,128)(2,1)} %fusion.12), channel_id=1, source_target_pairs={{0,1},{1,0},{2,3},{3,2},{4,5},{5,4},{6,7},{7,6},{8,9},{9,8},{10,11... | collective-permute-start | bytes 4718600 | tf_op jit(solution)/shard_map/ppermute | solution.py:297
  197.6 110.5 %collective-permute-start.27 = (bf16[8,96,1024]{2,1,0:T(8,128)(2,1)}, bf16[8,96,1024]{2,1,0:T(8,128)(2,1)}, u32[]{:S(2)}, u32[]{:S(2)}) collective-permute-start(bf16[8,96,1024]{2,1,0:T(8,128)(2,1)} %bitcast.98), channel_id=1, source_target_pairs={{0,8},{2,10},{4,12},{6,14},{8,0},{10,2},{12,4},{14,6},{16,24},{18,... | collective-permute-start | bytes 4718600 | tf_op jit(solution)/shard_map/ppermute | solution.py:261
  268.6 91.1 %collective-permute-start.36 = (bf16[4,96,1024]{2,1,0:T(8,128)(2,1)}, bf16[4,96,1024]{2,1,0:T(8,128)(2,1)}, u32[]{:S(2)}, u32[]{:S(2)}) collective-permute-start(bf16[4,96,1024]{2,1,0:T(8,128)(2,1)} %fusion.28), channel_id=1, source_target_pairs={{0,2},{2,0},{4,6},{6,4},{8,10},{10,8},{12,14},{14,12},{16,18},{18,... | collective-permute-start | bytes 2359304 | tf_op jit(solution)/shard_map/ppermute | solution.py:261
  294.8 66.6 %collective-permute-start.24 = (bf16[4,96,1024]{2,1,0:T(8,128)(2,1)S(1)}, bf16[4,96,1024]{2,1,0:T(8,128)(2,1)S(1)}, u32[]{:S(2)}, u32[]{:S(2)}) collective-permute-start(bf16[4,96,1024]{2,1,0:T(8,128)(2,1)S(1)} %copy-done.34), channel_id=1, source_target_pairs={{0,4},{2,6},{4,0},{6,2},{8,12},{10,14},{12,8},{14,10},{16,20},{18,... | collective-permute-start | bytes 2359304 | tf_op jit(solution)/shard_map/ppermute | solution.py:261
  321.0 21.0 %collective-permute-start.43 = (f32[1,6,48]{2,0,1:T(1,128)S(1)}, f32[1,6,48]{2,0,1:T(1,128)S(1)}, u32[]{:S(2)}, u32[]{:S(2)}) collective-permute-start(f32[1,6,48]{2,0,1:T(1,128)S(1)} %get-tuple-element.85), channel_id=1, source_target_pairs={{0,16},{2,18},{4,20},{6,22},{8,24},{10,26},{12,28},{14,30},{16,0},... | collective-permute-start | bytes 3464 | tf_op jit(solution)/shard_map/ppermute | solution.py:261
  342.6 64.9 %collective-permute-start.14 = (bf16[16,48,1536]{2,1,0:T(8,128)(2,1)S(1)}, bf16[16,48,1536]{2,1,0:T(8,128)(2,1)S(1)}, u32[]{:S(2)}, u32[]{:S(2)}) collective-permute-start(bf16[16,48,1536]{2,1,0:T(8,128)(2,1)S(1)} %copy-done.33), channel_id=1, source_target_pairs={{0,1},{1,0},{2,3},{3,2},{4,5},{5,4},{6,7},{7,6},{8,9},{9,8},{10,11... | collective-permute-start | bytes 7077896 | tf_op jit(solution)/shard_map/ppermute | solution.py:261
  344.2 47.6 %collective-permute-start.32 = (bf16[4,96,1536]{2,1,0:T(8,128)(2,1)S(1)}, bf16[4,96,1536]{2,1,0:T(8,128)(2,1)S(1)}, u32[]{:S(2)}, u32[]{:S(2)}) collective-permute-start(bf16[4,96,1536]{2,1,0:T(8,128)(2,1)S(1)} %fusion.23), channel_id=1, source_target_pairs={{0,4},{2,6},{4,0},{6,2},{8,12},{10,14},{12,8},{14,10},{16,20},{18,... | collective-permute-start | bytes 3538952 | tf_op jit(solution)/shard_map/ppermute | solution.py:261
  369.0 103.3 %collective-permute-start.9 = (bf16[16,48,2304]{2,1,0:T(8,128)(2,1)S(1)}, bf16[16,48,2304]{2,1,0:T(8,128)(2,1)S(1)}, u32[]{:S(2)}, u32[]{:S(2)}) collective-permute-start(bf16[16,48,2304]{2,1,0:T(8,128)(2,1)S(1)} %copy-done.27), channel_id=1, source_target_pairs={{0,1},{1,0},{2,3},{3,2},{4,5},{5,4},{6,7},{7,6},{8,9},{9,8},{10,11... | collective-permute-start | bytes 10616840 | tf_op jit(solution)/shard_map/ppermute | solution.py:261
  380.2 26.4 %collective-permute-start.20 = (bf16[4,96,1536]{2,1,0:T(8,128)(2,1)S(1)}, bf16[4,96,1536]{2,1,0:T(8,128)(2,1)S(1)}, u32[]{:S(2)}, u32[]{:S(2)}) collective-permute-start(bf16[4,96,1536]{2,1,0:T(8,128)(2,1)S(1)} %fusion.22), channel_id=1, source_target_pairs={{0,2},{2,0},{4,6},{6,4},{8,10},{10,8},{12,14},{14,12},{16,18},{18,... | collective-permute-start | bytes 3538952 | tf_op jit(solution)/shard_map/ppermute | solution.py:261
  390.8 82.6 %collective-permute-start.4 = (bf16[16,48,2304]{2,1,0:T(8,128)(2,1)S(1)}, bf16[16,48,2304]{2,1,0:T(8,128)(2,1)S(1)}, u32[]{:S(2)}, u32[]{:S(2)}) collective-permute-start(bf16[16,48,2304]{2,1,0:T(8,128)(2,1)S(1)} %copy-done.26), channel_id=1, source_target_pairs={{0,1},{1,0},{2,3},{3,2},{4,5},{5,4},{6,7},{7,6},{8,9},{9,8},{10,11... | collective-permute-start | bytes 10616840 | tf_op jit(solution)/shard_map/ppermute | solution.py:261
  406.8 32.0 %collective-permute-start.21 = (bf16[2,96,1536]{2,1,0:T(8,128)(2,1)S(1)}, bf16[2,96,1536]{2,1,0:T(8,128)(2,1)S(1)}, u32[]{:S(2)}, u32[]{:S(2)}) collective-permute-start(bf16[2,96,1536]{2,1,0:T(8,128)(2,1)S(1)} %fusion.30), channel_id=1, source_target_pairs={{0,8},{2,10},{4,12},{6,14},{8,0},{10,2},{12,4},{14,6},{16,24},{18,... | collective-permute-start | bytes 1769480 | tf_op jit(solution)/shard_map/ppermute | solution.py:261
  420.5 49.0 %collective-permute-start.15 = (bf16[8,48,1536]{2,1,0:T(8,128)(2,1)S(1)}, bf16[8,48,1536]{2,1,0:T(8,128)(2,1)S(1)}, u32[]{:S(2)}, u32[]{:S(2)}) collective-permute-start(bf16[8,48,1536]{2,1,0:T(8,128)(2,1)S(1)} %bitcast.469), channel_id=1, source_target_pairs={{0,8},{2,10},{4,12},{6,14},{8,0},{10,2},{12,4},{14,6},{16,24},{18,... | collective-permute-start | bytes 3538952 | tf_op jit(solution)/shard_map/ppermute | solution.py:261
  439.0 28.4 %collective-permute-start.22 = (bf16[1,96,1536]{2,1,0:T(8,128)(2,1)S(1)}, bf16[1,96,1536]{2,1,0:T(8,128)(2,1)S(1)}, u32[]{:S(2)}, u32[]{:S(2)}) collective-permute-start(bf16[1,96,1536]{2,1,0:T(8,128)(2,1)S(1)} %fusion.33), channel_id=1, source_target_pairs={{0,16},{2,18},{4,20},{6,22},{8,24},{10,26},{12,28},{14,30},{16,0},... | collective-permute-start | bytes 884744 | tf_op jit(solution)/shard_map/ppermute | solution.py:261
  469.8 28.2 %collective-permute-start.16 = (bf16[4,48,1536]{2,1,0:T(8,128)(2,1)S(1)}, bf16[4,48,1536]{2,1,0:T(8,128)(2,1)S(1)}, u32[]{:S(2)}, u32[]{:S(2)}) collective-permute-start(bf16[4,48,1536]{2,1,0:T(8,128)(2,1)S(1)} %fusion.29), channel_id=1, source_target_pairs={{0,16},{2,18},{4,20},{6,22},{8,24},{10,26},{12,28},{14,30},{16,0},... | collective-permute-start | bytes 1769480 | tf_op jit(solution)/shard_map/ppermute | solution.py:261
  472.7 48.6 %collective-permute-start.10 = (bf16[8,48,2304]{2,1,0:T(8,128)(2,1)S(1)}, bf16[8,48,2304]{2,1,0:T(8,128)(2,1)S(1)}, u32[]{:S(2)}, u32[]{:S(2)}) collective-permute-start(bf16[8,48,2304]{2,1,0:T(8,128)(2,1)S(1)} %bitcast.456), channel_id=1, source_target_pairs={{0,4},{2,6},{4,0},{6,2},{8,12},{10,14},{12,8},{14,10},{16,20},{18,... | collective-permute-start | bytes 5308424 | tf_op jit(solution)/shard_map/ppermute | solution.py:261
  473.9 48.5 %collective-permute-start.5 = (bf16[8,48,2304]{2,1,0:T(8,128)(2,1)S(1)}, bf16[8,48,2304]{2,1,0:T(8,128)(2,1)S(1)}, u32[]{:S(2)}, u32[]{:S(2)}) collective-permute-start(bf16[8,48,2304]{2,1,0:T(8,128)(2,1)S(1)} %fusion.21), channel_id=1, source_target_pairs={{0,2},{2,0},{4,6},{6,4},{8,10},{10,8},{12,14},{14,12},{16,18},{18,... | collective-permute-start | bytes 5308424 | tf_op jit(solution)/shard_map/ppermute | solution.py:261
  498.1 21.6 %collective-permute-start.17 = (bf16[2,48,1536]{2,1,0:T(8,128)(2,1)S(1)}, bf16[2,48,1536]{2,1,0:T(8,128)(2,1)S(1)}, u32[]{:S(2)}, u32[]{:S(2)}) collective-permute-start(bf16[2,48,1536]{2,1,0:T(8,128)(2,1)S(1)} %fusion.44), channel_id=1, source_target_pairs={{0,2},{2,0},{4,6},{6,4},{8,10},{10,8},{12,14},{14,12},{16,18},{18,... | collective-permute-start | bytes 884744 | tf_op jit(solution)/shard_map/ppermute | solution.py:261
  519.9 23.9 %collective-permute-start.18 = (bf16[1,48,1536]{2,1,0:T(8,128)(2,1)S(1)}, bf16[1,48,1536]{2,1,0:T(8,128)(2,1)S(1)}, u32[]{:S(2)}, u32[]{:S(2)}) collective-permute-start(bf16[1,48,1536]{2,1,0:T(8,128)(2,1)S(1)} %fusion.46), channel_id=1, source_target_pairs={{0,4},{2,6},{4,0},{6,2},{8,12},{10,14},{12,8},{14,10},{16,20},{18,... | collective-permute-start | bytes 442376 | tf_op jit(solution)/shard_map/ppermute | solution.py:261
  522.7 20.7 %collective-permute-start.6 = (bf16[4,48,2304]{2,1,0:T(8,128)(2,1)S(1)}, bf16[4,48,2304]{2,1,0:T(8,128)(2,1)S(1)}, u32[]{:S(2)}, u32[]{:S(2)}) collective-permute-start(bf16[4,48,2304]{2,1,0:T(8,128)(2,1)S(1)} %fusion.24), channel_id=1, source_target_pairs={{0,4},{2,6},{4,0},{6,2},{8,12},{10,14},{12,8},{14,10},{16,20},{18,... | collective-permute-start | bytes 2654216 | tf_op jit(solution)/shard_map/ppermute | solution.py:261
  (88 other events, 908.5 us)
